TPU v7x, 512 devices: a whole 4x8x8 slice. The times are simulated.
512 devices in a mesh: dp: 128 (over z, y, core), mp: 4 (over x).
Axes of the slice: x: 4, y: 8, z: 8, core: 2. Of those that a mesh axis runs over, the one named last changes fastest.
Arguments:
- grad_out: bfloat16 [32768, 2304], P(('dp', 'mp')), may hold values from -6 to 6
- queries: bfloat16 [32768, 1536], P('dp', 'mp'), may hold values from -8 to 8
- keys: bfloat16 [4096, 1536], P('dp', 'mp'), may hold values from -8 to 8
- values: bfloat16 [4096, 1536], P('dp', 'mp'), may hold values from -6 to 6
- out_weight: bfloat16 [1536, 2304], P('mp'), may hold values from -0.15625 to 0.15625
- counts: int32 [128], P('dp'), may hold values from 0 to 4, as said below
- source: int32 [512], P('dp'), may hold values from 0 to 127, as said below
- offsets: int32 [512], P('dp'), may hold values from 0 to 16
- key_mask: int32 [512, 16], P('dp'), may hold values from 0 to 1, as said below
Outputs:
- query_grad: bfloat16 [32768, 1536], P('dp', 'mp')
- key_grad: bfloat16 [4096, 1536], P('dp', 'mp')
- value_grad: bfloat16 [4096, 1536], P('dp', 'mp')
- weight_grad: float32 [2304, 1536], P('dp', 'mp')
Inputs may be any that keep to these rules, and one draw needn't show every extreme that they name: The live image slots of a rank are its first counts slots; the counts of all ranks sum to 128. `source`: the live image slots of all ranks name every rank exactly once; entries of slots that are not live are arbitrary. `key_mask`: the rows of an image's block that are not padding come first, and there are at least 8 of them.
All inputs are finite; a program needn't handle non-finite values.
Results may differ from a plain program's by a relative error of at most 0.04.
Values may be sent and summed in bfloat16 or wider, within the bound.
A program may use at most 64 MiB of HBM per device.

v0:
```python
import jax
import jax.numpy as jnp
from jax import lax
from jax.sharding import PartitionSpec as P

HEAD_DIM = 128


def pick_rows(carry, pieces, row_ids):
    count = pieces[0].shape[0]
    inside = (row_ids >= 0) & (row_ids < count)
    safe = jnp.clip(row_ids, 0, count - 1).reshape(-1)
    result = []
    for held, piece in zip(carry, pieces):
        taken = jnp.take(piece, safe, axis=0).reshape(held.shape)
        result.append(jnp.where(inside[:, :, None], taken, held))
    return tuple(result)


def on_device(grad_out, queries, keys, values, out_weight, counts, source, offsets, key_mask):
    scale = HEAD_DIM ** (-0.5)
    slots = source.shape[0]
    cond = key_mask.shape[1]
    own_rows = keys.shape[0]
    width = queries.shape[1]
    heads_here = width // HEAD_DIM
    patches = queries.shape[0] // slots
    group_size = lax.axis_size("dp")
    device = lax.axis_index("dp")
    upstream = lax.all_gather(grad_out, "mp", axis=0, tiled=True)
    grad_attn = lax.dot_general(
        upstream, out_weight, (((1,), (1,)), ((), ())), preferred_element_type=jnp.float32
    ).astype(jnp.bfloat16)
    every_source, every_offset, every_count = (
        lax.all_gather(source, "dp", axis=0, tiled=True),
        lax.all_gather(offsets, "dp", axis=0, tiled=True),
        lax.all_gather(counts, "dp", axis=0, tiled=True),
    )
    every_live = (jnp.arange(slots)[None, :] < every_count[:, None]).reshape(-1)
    claims = every_live & (every_source == device)
    own_offset = jnp.sum(jnp.where(claims, every_offset, 0))
    served = jnp.any(claims)
    live = jnp.arange(slots) < counts[0]
    empty = jnp.zeros((slots, cond, width), jnp.bfloat16)
    spans = jnp.arange(cond)[None, :]
    shard_ids = source[:, None] * own_rows + offsets[:, None] + spans
    key_blocks, value_blocks = pick_rows(
        (empty, empty),
        (
            lax.all_gather(keys, "dp", axis=0, tiled=True),
            lax.all_gather(values, "dp", axis=0, tiled=True),
        ),
        shard_ids,
    )
    query_blocks = queries.reshape(slots, patches, heads_here, HEAD_DIM)
    grad_blocks = grad_attn.reshape(slots, patches, heads_here, HEAD_DIM)
    key_heads = key_blocks.reshape(slots, cond, heads_here, HEAD_DIM)
    value_heads = value_blocks.reshape(slots, cond, heads_here, HEAD_DIM)
    live_four = live[:, None, None, None]
    scores = (
        jnp.einsum("sqhd,skhd->shkq", query_blocks, key_heads, preferred_element_type=jnp.float32)
        * scale
    )
    scores = jnp.where(key_mask[:, None, :, None] > 0, scores, -jnp.inf)
    highest = jnp.max(scores, axis=2, keepdims=True)
    expos = jnp.exp(scores - highest)
    probs = expos / jnp.sum(expos, axis=2, keepdims=True)
    probs_b = probs.astype(jnp.bfloat16)
    attended = jnp.einsum(
        "shkq,skhd->sqhd", probs_b, value_heads, preferred_element_type=jnp.float32
    )
    attended = jnp.where(live_four, attended, 0.0).astype(jnp.bfloat16)
    delta = jnp.einsum("sqhd,sqhd->sqh", grad_blocks, attended, preferred_element_type=jnp.float32)
    dprob = jnp.einsum(
        "sqhd,skhd->shkq", grad_blocks, value_heads, preferred_element_type=jnp.float32
    )
    dscore = (probs * (dprob - jnp.transpose(delta, (0, 2, 1))[:, :, None, :])).astype(jnp.bfloat16)
    query_grad = (
        jnp.einsum("shkq,skhd->sqhd", dscore, key_heads, preferred_element_type=jnp.float32) * scale
    )
    query_grad = (
        jnp.where(live_four, query_grad, 0.0).astype(jnp.bfloat16).reshape(slots * patches, width)
    )
    key_part = (
        jnp.einsum("shkq,sqhd->skhd", dscore, query_blocks, preferred_element_type=jnp.float32)
        * scale
    )
    key_part = jnp.where(live_four, key_part, 0.0).astype(jnp.bfloat16).reshape(slots, cond, width)
    value_part = jnp.einsum(
        "shkq,sqhd->skhd", probs_b, grad_blocks, preferred_element_type=jnp.float32
    )
    value_part = (
        jnp.where(live_four, value_part, 0.0).astype(jnp.bfloat16).reshape(slots, cond, width)
    )
    routes = (live[:, None] & (source[:, None] == jnp.arange(group_size)[None, :])).astype(
        jnp.bfloat16
    )
    send_key_grads = jnp.einsum(
        "sp,skc->pkc", routes, key_part, preferred_element_type=jnp.float32
    ).astype(jnp.bfloat16)
    send_value_grads = jnp.einsum(
        "sp,skc->pkc", routes, value_part, preferred_element_type=jnp.float32
    ).astype(jnp.bfloat16)
    back_keys, back_values = (
        lax.all_to_all(send_key_grads, "dp", split_axis=0, concat_axis=0, tiled=True),
        lax.all_to_all(send_value_grads, "dp", split_axis=0, concat_axis=0, tiled=True),
    )
    key_window_grad = jnp.where(served, jnp.sum(back_keys.astype(jnp.float32), axis=0), 0.0).astype(
        jnp.bfloat16
    )
    value_window_grad = jnp.where(
        served, jnp.sum(back_values.astype(jnp.float32), axis=0), 0.0
    ).astype(jnp.bfloat16)
    blank = jnp.zeros((own_rows, width), jnp.bfloat16)
    key_grad = lax.dynamic_update_slice_in_dim(blank, key_window_grad, own_offset, 0)
    value_grad = lax.dynamic_update_slice_in_dim(blank, value_window_grad, own_offset, 0)
    attended_rows = attended.reshape(slots * patches, width)
    weight_grad = lax.psum_scatter(
        lax.dot_general(
            upstream, attended_rows, (((0,), (0,)), ((), ())), preferred_element_type=jnp.float32
        ),
        "dp",
        scatter_dimension=0,
        tiled=True,
    )
    return (query_grad, key_grad, value_grad, weight_grad)


def solution(mesh):
    in_specs = (
        P(("dp", "mp"), None),
        P("dp", "mp"),
        P("dp", "mp"),
        P("dp", "mp"),
        P("mp", None),
        P("dp"),
        P("dp"),
        P("dp"),
        P("dp", None),
    )
    out_specs = (P("dp", "mp"), P("dp", "mp"), P("dp", "mp"), P("dp", "mp"))
    return jax.shard_map(
        on_device, mesh=mesh, in_specs=in_specs, out_specs=out_specs, check_vma=False
    )
```

profile of v0, /device:TPU:1, one launch (start us, length us, event | category | flops | bytes accessed | tf_op | source)
XLA Modules:
  0.0 517.1 jit_solution(12320781244733669975)
XLA Ops:
  10.9 1.0 reshape.94
  12.7 31.7 %all-gather.8.cloned.1.call-done = bf16[256,2304]{1,0:T(8,128)(2,1)} async-done(((bf16[64,2304]{1,0:T(8,128)(2,1)}), bf16[256,2304]{1,0:T(8,128)(2,1)}) %all-gather.8.cloned.1.call-update) | async-done | bytes 1179664 | tf_op jit(solution)/shard_map/all_gather | solution.py:30
  44.4 2.1 convolution_convert_fusion.2
  46.6 86.8 %all-gather.4.cloned.1.call-done = bf16[4096,384]{1,0:T(8,128)(2,1)} async-done(((bf16[32,384]{1,0:T(8,128)(2,1)}), bf16[4096,384]{1,0:T(8,128)(2,1)}) %all-gather.4.cloned.1.call-update) | async-done | bytes 3145744 | tf_op jit(solution)/shard_map/all_gather | solution.py:50
  133.4 3.0 gather_fusion
  136.4 80.9 %all-gather.6.cloned.1.call-done = bf16[4096,384]{1,0:T(8,128)(2,1)} async-done(((bf16[32,384]{1,0:T(8,128)(2,1)}), bf16[4096,384]{1,0:T(8,128)(2,1)}) %all-gather.6.cloned.1.call-update) | async-done | bytes 3145744 | tf_op jit(solution)/shard_map/all_gather | solution.py:51
  217.3 3.0 gather_fusion.1
  222.5 2.1 copy.49
  224.6 9.6 %all-to-all-start.1 = ((bf16[128,16,384]{2,1,0:T(8,128)(2,1)}), bf16[128,16,384]{2,1,0:T(8,128)(2,1)S(1)}, u32[]{:S(2)}, u32[]{:S(2)}) async-start(bf16[128,16,384]{2,1,0:T(8,128)(2,1)} %copy.49), calls=%async_computation.1 | async-start | bytes 3145728 | tf_op jit(solution)/shard_map/all_to_all | solution.py:106
  234.2 1.1 bitcast_convert_fusion
  235.3 1.5 multiply_reduce_fusion
  236.8 1.2 fusion.12
  238.7 1.1 fusion.14
  239.9 1.4 convolution_convert_fusion.1
  241.3 2.1 copy.45
  243.4 32.0 %all-to-all-done.1 = bf16[128,16,384]{2,1,0:T(8,128)(2,1)S(1)} async-done(((bf16[128,16,384]{2,1,0:T(8,128)(2,1)}), bf16[128,16,384]{2,1,0:T(8,128)(2,1)S(1)}, u32[]{:S(2)}, u32[]{:S(2)}) %all-to-all-start.1) | async-done | bytes 1572896 | tf_op jit(solution)/shard_map/all_to_all | solution.py:106
  275.4 7.9 %all-to-all-start = ((bf16[128,16,384]{2,1,0:T(8,128)(2,1)}), bf16[128,16,384]{2,1,0:T(8,128)(2,1)}, u32[]{:S(2)}, u32[]{:S(2)}) async-start(bf16[128,16,384]{2,1,0:T(8,128)(2,1)} %copy.45), calls=%async_computation | async-start | bytes 3145728 | tf_op jit(solution)/shard_map/all_to_all | solution.py:105
  283.8 3.7 convolution_bitcast_fusion
  289.9 0.8 dynamic-update-slice
  290.6 46.1 %all-reduce.4 = (s32[128]{0:T(128)S(1)}, s32[512]{0:T(512)S(1)}, s32[512]{0:T(512)S(1)}) all-reduce(s32[128]{0:T(128)S(1)} %dynamic-update-slice, s32[512]{0:T(512)S(1)} %dynamic-update-slice.1, s32[512]{0:T(512)S(1)} %dynamic-update-slice.2), channel_id=1, replica_groups=mesh['dp'=128,'mp'=4] {'dp'}, use_global_device_ids=true, to_apply=%add | all-reduce | flops 1152 | bytes 9216
  342.0 162.3 %all-reduce.7.cloned.1.call-done = f32[2304,384]{0,1:T(8,128)} async-done(((f32[2304,384]{0,1:T(8,128)}), f32[2304,384]{0,1:T(8,128)}) %all-reduce.7.cloned.1.call-update) | async-done | bytes 3538960
  504.2 1.1 constant_dynamic-slice_fusion
  505.4 0.7 copy.51
  507.0 1.7 convert_reduce_fusion.1
  (85 shorter events, 14.3 us)
Async XLA Ops:
  7.2 37.3 %copy-start = (bf16[384,2304]{1,0:T(8,128)(2,1)S(1)}, bf16[384,2304]{1,0:T(8,128)(2,1)}, u32[]{:S(2)}) copy-start(bf16[384,2304]{1,0:T(8,128)(2,1)} %param.15) | copy-start | bytes 5308420
  7.2 37.3 %all-gather.8.cloned.1.call-start = ((), (), s32[]{:S(2)}) async-start(), calls=%async_computation.4 | async-start | bytes 1474560 | tf_op jit(solution)/shard_map/all_gather | solution.py:30
  7.9 125.4 %all-gather.4.cloned.1.call-start = ((), (), s32[]{:S(2)}) async-start(), calls=%async_computation.2 | async-start | bytes 3170304 | tf_op jit(solution)/shard_map/all_gather | solution.py:50
  8.7 208.6 %all-gather.6.cloned.1.call-start = ((), (), s32[]{:S(2)}) async-start(), calls=%async_computation.3 | async-start | bytes 3170304 | tf_op jit(solution)/shard_map/all_gather | solution.py:51
  11.9 208.7 %copy-start.2 = (bf16[4,64,3,128]{3,2,1,0:T(4,128)(2,1)}, bf16[4,64,3,128]{3,2,1,0:T(4,128)(2,1)S(1)}, u32[]{:S(2)}) copy-start(bf16[4,64,3,128]{3,2,1,0:T(4,128)(2,1)S(1)} %reshape.94) | copy-start | bytes 589828
  11.9 222.3 %copy-start.10 = (pred[4]{0:T(512)(128)(4,1)}, pred[4]{0:T(512)(128)(4,1)S(1)}, u32[]{:S(2)}) copy-start(pred[4]{0:T(512)(128)(4,1)S(1)} %iota_compare_fusion.2) | copy-start | bytes 16
  46.6 175.9 %copy-start.1 = (bf16[4,64,3,128]{3,2,1,0:T(4,128)(2,1)}, bf16[4,64,3,128]{3,2,1,0:T(4,128)(2,1)S(1)}, u32[]{:S(2)}) copy-start(bf16[4,64,3,128]{3,2,1,0:T(4,128)(2,1)S(1)} %reshape.96) | copy-start | bytes 589828
  46.6 175.2 %copy-start.8 = (s32[4]{0:T(128)S(1)}, s32[4]{0:T(128)}, u32[]{:S(2)}) copy-start(s32[4]{0:T(128)} %param.17) | copy-start | bytes 52
  220.6 4.0 copy-start.4
  224.6 50.8 %all-to-all-start.1 = ((bf16[128,16,384]{2,1,0:T(8,128)(2,1)}), bf16[128,16,384]{2,1,0:T(8,128)(2,1)S(1)}, u32[]{:S(2)}, u32[]{:S(2)}) async-start(bf16[128,16,384]{2,1,0:T(8,128)(2,1)} %copy.49), calls=%async_computation.1 | async-start | bytes 3145728 | tf_op jit(solution)/shard_map/all_to_all | solution.py:106
  238.0 0.6 copy-start.14
  243.4 40.2 %copy-start.3 = (bf16[4,3,128,64]{2,3,1,0:T(8,128)(2,1)S(1)}, bf16[4,3,128,64]{2,3,1,0:T(8,128)(2,1)}, u32[]{:S(2)}) copy-start(bf16[4,3,128,64]{2,3,1,0:T(8,128)(2,1)} %get-tuple-element.31) | copy-start | bytes 589828
  275.4 231.6 %all-to-all-start = ((bf16[128,16,384]{2,1,0:T(8,128)(2,1)}), bf16[128,16,384]{2,1,0:T(8,128)(2,1)}, u32[]{:S(2)}, u32[]{:S(2)}) async-start(bf16[128,16,384]{2,1,0:T(8,128)(2,1)} %copy.45), calls=%async_computation | async-start | bytes 3145728 | tf_op jit(solution)/shard_map/all_to_all | solution.py:105
  283.3 220.9 %all-reduce.7.cloned.1.call-start = ((), (), s32[]{:S(2)}) async-start(), calls=%async_computation.5 | async-start | bytes 7077888
  287.5 0.7 copy-start.12
  287.5 1.9 copy-start.9
  287.5 2.2 copy-start.13
  287.5 53.3 %copy-start.5 = (bf16[4,16,3,128]{3,2,1,0:T(4,128)(2,1)S(1)}, bf16[4,16,3,128]{3,2,1,0:T(4,128)(2,1)}, u32[]{:S(2)}) copy-start(bf16[4,16,3,128]{3,2,1,0:T(4,128)(2,1)} %copy-done.4) | copy-start | bytes 147460
  287.5 53.3 %copy-start.11 = (pred[4]{0:T(512)(128)(4,1)S(1)}, pred[4]{0:T(512)(128)(4,1)}, u32[]{:S(2)}) copy-start(pred[4]{0:T(512)(128)(4,1)} %copy-done.10) | copy-start | bytes 16
  287.5 53.3 %copy-start.15 = (bf16[4,3,16,64]{3,2,1,0:T(8,128)(2,1)S(1)}, bf16[4,3,16,64]{3,2,1,0:T(8,128)(2,1)}, u32[]{:S(2)}) copy-start(bf16[4,3,16,64]{3,2,1,0:T(8,128)(2,1)} %copy-done.14) | copy-start | bytes 73732
  509.7 0.6 copy-start.7
  510.0 0.6 copy-start.6
Sparse Core Ops, SparseCore 0:
  10.1 34.2 all-gather.7
  47.6 85.7 all-gather.3
  136.5 80.7 all-gather.5
  287.6 216.5 all-reduce.6
where the time goes:
time: 519 us; the launch traced here: 517 us
  waiting for transfers between devices  396 us (76%)
  blocking collectives  46.1 us (9%)
  local copies, waits for them, and re-layouts  18.9 us (4%)
  between operations  18.1 us (3%)
  starting transfers between devices  17.8 us (3%)
  matrix products  11.9 us (2%)
  other arithmetic  8.56 us (2%)
    unnamed x5, waiting for transfers between devices  164 us
    all_gather x1, waiting for transfers between devices, on_device(): lax.all_gather(keys, 'dp', axis=0, tiled=True)  86.8 us
    all_gather x1, waiting for transfers between devices, on_device(): lax.all_gather(values, 'dp', axis=0, tiled=True)  80.9 us
    unnamed x1, blocking collectives  46.1 us
    all_to_all x1, waiting for transfers between devices, on_device(): lax.all_to_all(send_value_grads, 'dp', split_axis=0, concat_axis=0, tiled...  32 us
    all_gather x1, waiting for transfers between devices, on_device(): upstream = lax.all_gather(grad_out, 'mp', axis=0, tiled=True)  31.7 us
  transfers between devices with their start and end apart: 6, of which 5 were waited for; matrix products, arithmetic and copies ran while one was open for 5% of the time, Pallas kernels for 0%

commit v1 on v0

v1 whole, which is shorter than its diff:
```python
import functools

import jax
import jax.numpy as jnp
from jax import lax
from jax.experimental import pallas as pl
from jax.experimental.pallas import tpu as pltpu
from jax.sharding import PartitionSpec as P

HEAD_DIM = 128
NZ, NY, NC, NX = 8, 8, 2, 4
MESH = pl.DeviceIdType.MESH
F32, BF16, I32 = jnp.float32, jnp.bfloat16, jnp.int32
NN = (((1,), (0,)), ((), ()))
NT = (((1,), (1,)), ((), ()))
TN = (((0,), (0,)), ((), ()))


def dot(a, b, dims):
    return lax.dot_general(a, b, dims, preferred_element_type=F32)


def total(ref, slots):
    acc = ref[0].astype(F32)
    for i in range(1, slots):
        acc = acc + ref[i].astype(F32)
    return acc


def kernel(
    counts, source, offsets, mask, g_hbm, q_hbm, k_hbm, v_hbm, w_hbm,
    qg_out, kg_out, vg_out, wg_out,
    q_v, w_v, g_all, g_other, gt,
    k_rows, v_rows, meta_z, meta_y, pick_k, pick_v,
    k_sel, v_sel, k_in, v_in,
    att, att_other, k_back, v_back, k_spread, v_spread, k_other, v_other,
    k_send, v_send, k_last, v_last,
    w_part, w_send, w_in, w_pad, w_last,
    local_sem, pair_send, pair_recv, x_send, x_recv, z_send, z_recv, y_send, y_recv,
):
    scale = HEAD_DIM ** -0.5
    dp, x = lax.axis_index("dp"), lax.axis_index("mp")
    z, y, c = lax.div(dp, NY * NC), lax.rem(lax.div(dp, NC), NY), lax.rem(dp, NC)
    slots, patches, cond, own = 4, 64, 16, 32
    width = q_v.shape[1]
    heads = width // HEAD_DIM

    def place(z, y, c, x):
        return ((z * NY + y) * NC + c, x)

    z_at = [lax.rem(z + k, NZ) for k in range(NZ)]
    y_at = [lax.rem(y + k, NY) for k in range(NY)]
    z_peer = [place(z_at[k], y, c, x) for k in range(NZ)]
    y_peer = [place(z, y_at[k], c, x) for k in range(NY)]
    x_peer = [place(z, y, c, lax.rem(x + k, NX)) for k in range(NX)]
    pair = place(z, y, 1 - c, x)

    started = []

    def push(src, dst, send, recv, device):
        copy = pltpu.make_async_remote_copy(
            src_ref=src, dst_ref=dst, send_sem=send, recv_sem=recv,
            device_id=device, device_id_type=MESH,
        )
        copy.start()
        started.append(copy)
        return copy

    def along_z(line, source_of, dst):
        return [
            push(source_of(k), dst.at[z], z_send.at[line, k], z_recv.at[line, k], z_peer[k])
            for k in range(1, NZ)
        ]

    def along_y(line, source_of, dst):
        return [
            push(source_of(k), dst.at[y], y_send.at[line, k], y_recv.at[line, k], y_peer[k])
            for k in range(1, NY)
        ]

    def across(line, src, dst):
        return push(src, dst, pair_send.at[line], pair_recv.at[line], pair)

    def arrive(copies):
        for copy in copies:
            copy.wait_recv()

    def load(i, src, dst):
        copy = pltpu.make_async_copy(src, dst, local_sem.at[i])
        copy.start()
        return copy

    load_k = load(0, k_hbm, k_rows.at[c, y])
    load_v = load(1, v_hbm, v_rows.at[c, z])
    load_g = load(2, g_hbm, g_all.at[x])
    load_q = load(3, q_hbm, q_v)
    load_w = load(4, w_hbm, w_v)

    lane = lax.broadcasted_iota(I32, (8, 128), 1)
    slot, row = (lane >> 4) & 3, lane & 15
    rows_named = jnp.full((8, 128), -(1 << 20), I32)
    for j in range(slots):
        first = jnp.where(j < counts[0], source[j] * own + offsets[j], -(1 << 20))
        rows_named = jnp.where(slot == j, first + row, rows_named)
    meta_z[z] = rows_named
    meta_y[y] = rows_named

    barrier = pltpu.get_barrier_semaphore()
    for device in [pair] + x_peer[1:] + z_peer[1:] + y_peer[1:]:
        pl.semaphore_signal(barrier, inc=1, device_id=device, device_id_type=MESH)
    pl.semaphore_wait(barrier, 1 + (NX - 1) + (NZ - 1) + (NY - 1))

    k_rows_sent = along_y(0, lambda k: k_hbm, k_rows.at[c])
    v_rows_sent = along_z(0, lambda k: v_hbm, v_rows.at[c])
    x_sent = [
        push(g_hbm, g_all.at[x], x_send.at[k], x_recv.at[k], x_peer[k]) for k in range(1, NX)
    ]
    meta_z_sent = along_z(1, lambda k: meta_z.at[z], meta_z)
    meta_y_sent = along_y(1, lambda k: meta_y.at[y], meta_y)
    g_pair = [across(0, g_hbm, g_other.at[x])]

    arrive(meta_z_sent)
    arrive(meta_y_sent)
    in_first = lax.broadcasted_iota(I32, (1, 128), 1) < 64
    rows_of = lax.broadcasted_iota(I32, (NC * NZ * own, 128), 0)

    def one_hot(meta, along, keep, pick):
        for p in range(4):
            ids = jnp.where(in_first, meta[2 * p, 0:1, :], meta[2 * p + 1, 0:1, :])
            local = ((ids >> 5) & 1) * (8 * own) + along(ids) * own + (ids & (own - 1))
            local = jnp.where(keep(ids), local, -1)
            pick[:, 128 * p : 128 * (p + 1)] = jnp.where(rows_of == local, 1.0, 0.0).astype(BF16)

    one_hot(meta_z, lambda i: (i >> 6) & 7, lambda i: (i >> 9) == z, pick_k)
    one_hot(meta_y, lambda i: i >> 9, lambda i: (i >= 0) & (((i >> 6) & 7) == y), pick_v)

    load_k.wait()
    arrive(k_rows_sent)
    k_pair = across(1, k_rows.at[c], k_rows.at[c])
    load_v.wait()
    arrive(v_rows_sent)
    v_pair = across(2, v_rows.at[c], v_rows.at[c])

    k_pair.wait_recv()
    k_sel[...] = (
        dot(pick_k[...], k_rows[...].reshape(512, width), TN).astype(BF16).reshape(8, 64, width)
    )
    k_in_sent = along_z(2, lambda k: k_sel.at[z_at[k]], k_in)
    k_in[z] = k_sel[z]
    v_pair.wait_recv()
    v_sel[...] = (
        dot(pick_v[...], v_rows[...].reshape(512, width), TN).astype(BF16).reshape(8, 64, width)
    )
    v_in_sent = along_y(2, lambda k: v_sel.at[y_at[k]], v_in)
    v_in[y] = v_sel[y]

    for k in range(1, NX):
        x_sent[k - 1].wait_recv()
        came = lax.rem(x + NX - k, NX)
        g_pair.append(across(2 + k, g_all.at[came], g_other.at[came]))
    load_g.wait()
    load_w.wait()
    load_q.wait()
    g = g_all[...].reshape(slots * patches, -1)
    ga = dot(g, w_v[...], NT).astype(BF16)
    gt[:, 0:256] = g.T
    arrive(g_pair)
    gt[:, 256:512] = g_other[...].reshape(slots * patches, -1).T

    eye = lax.broadcasted_iota(I32, (cond, cond), 0) == lax.broadcasted_iota(I32, (cond, cond), 1)
    kept = jnp.concatenate(
        [
            jnp.sum(jnp.where(eye, mask[s : s + 1, :].astype(F32), 0.0), axis=1, keepdims=True)
            for s in range(slots)
        ],
        axis=0,
    )
    same_slot = (lax.broadcasted_iota(I32, (64, 256), 0) >> 4) == (
        lax.broadcasted_iota(I32, (64, 256), 1) >> 6
    )

    def grouped(a, op):
        a = a.reshape(slots, cond, 256)
        a = op(a, axis=1, keepdims=True)
        return jnp.broadcast_to(a, (slots, cond, 256)).reshape(64, 256)

    arrive(k_in_sent)
    k_blocks = total(k_in, NZ).astype(BF16)
    q = q_v[...]
    probs = []
    for h in range(heads):
        cols = slice(h * HEAD_DIM, (h + 1) * HEAD_DIM)
        scores = dot(k_blocks[:, cols], q[:, cols], NT) * scale
        scores = jnp.where(kept > 0.5, scores, -1e30)
        expos = jnp.exp(scores - grouped(scores, jnp.max))
        probs.append(jnp.where(same_slot, expos / grouped(expos, jnp.sum), 0.0))
    arrive(v_in_sent)
    v_blocks = total(v_in, NY).astype(BF16)
    for h in range(heads):
        cols = slice(h * HEAD_DIM, (h + 1) * HEAD_DIM)
        att[:, cols] = dot(probs[h].astype(BF16), v_blocks[:, cols], TN).astype(BF16)
    att_pair = across(6, att, att_other)

    dscores = []
    for h in range(heads):
        cols = slice(h * HEAD_DIM, (h + 1) * HEAD_DIM)
        probs_b = probs[h].astype(BF16)
        dprob = dot(v_blocks[:, cols], ga[:, cols], NT)
        delta = grouped(probs_b.astype(F32) * dprob, jnp.sum)
        dscore = (probs[h] * (dprob - delta)).astype(BF16)
        dscores.append(dscore)
        k_back[z, :, cols] = (dot(dscore, q[:, cols], NN) * scale).astype(BF16)
        v_back[y, :, cols] = dot(probs_b, ga[:, cols], NN).astype(BF16)
    k_back_sent = along_z(3, lambda k: k_back.at[z], k_back)
    v_back_sent = along_y(3, lambda k: v_back.at[y], v_back)

    att_pair.wait_recv()
    for b in range(6):
        rows = slice(b * 384, (b + 1) * 384)
        part = dot(gt[rows, 0:256], att[...], NN) + dot(gt[rows, 256:512], att_other[...], NN)
        w_part[rows, :] = part.astype(BF16)
    i = lax.broadcasted_iota(I32, (144, 288), 0)
    parity = jnp.where(
        lax.broadcasted_iota(I32, (144, 288), 1) == i + 18 * ((i * 3641) >> 16) + 18 * c, 1.0, 0.0
    ).astype(BF16)
    for b in range(NZ):
        w_send[b] = dot(parity, w_part[b * 288 : (b + 1) * 288, :], NN).astype(BF16)
    w_sent = along_z(4, lambda k: w_send.at[z_at[k]], w_in)
    w_in[z] = w_send[z]

    for h in range(heads):
        cols = slice(h * HEAD_DIM, (h + 1) * HEAD_DIM)
        qg_out[:, cols] = (dot(dscores[h], k_blocks[:, cols], TN) * scale).astype(BF16)

    arrive(k_back_sent)
    k_spread[...] = (
        dot(pick_k[...], k_back[...].reshape(512, width), NN).astype(BF16).reshape(2, 8, own, width)
    )
    k_swap = across(7, k_spread.at[1 - c], k_other)
    arrive(v_back_sent)
    v_spread[...] = (
        dot(pick_v[...], v_back[...].reshape(512, width), NN).astype(BF16).reshape(2, 8, own, width)
    )
    v_swap = across(8, v_spread.at[1 - c], v_other)
    k_swap.wait_recv()
    k_send[...] = k_spread[c] + k_other[...]
    k_last_sent = along_y(4, lambda k: k_send.at[y_at[k]], k_last)
    k_last[y] = k_send[y]
    v_swap.wait_recv()
    v_send[...] = v_spread[c] + v_other[...]
    v_last_sent = along_z(5, lambda k: v_send.at[z_at[k]], v_last)
    v_last[z] = v_send[z]

    arrive(w_sent)
    summed = total(w_in, NZ).astype(BF16)
    o = lax.broadcasted_iota(I32, (256, 144), 0)
    spread = jnp.where(
        ((o & 31) < 18) & (lax.broadcasted_iota(I32, (256, 144), 1) == (o >> 5) * 18 + (o & 31)),
        1.0, 0.0,
    ).astype(BF16)
    w_pad[...] = dot(spread, summed, NN).astype(BF16).reshape(8, 32, width)
    w_last_sent = along_y(5, lambda k: w_pad.at[y_at[k]], w_last)
    w_last[y] = w_pad[y]

    arrive(k_last_sent)
    kg_out[...] = total(k_last, NY).astype(BF16)
    arrive(v_last_sent)
    vg_out[...] = total(v_last, NZ).astype(BF16)
    arrive(w_last_sent)
    wg_out[...] = total(w_last, NY)[0:18, :]
    for copy in started:
        copy.wait_send()


def on_device(grad_out, queries, keys, values, out_weight, counts, source, offsets, key_mask):
    patches, d = grad_out.shape
    tokens, width = queries.shape
    own = keys.shape[0]
    vmem = lambda *shape, dtype=BF16: pltpu.VMEM(shape, dtype)
    smem = pl.BlockSpec(memory_space=pltpu.SMEM)
    whole = pl.BlockSpec(memory_space=pltpu.VMEM)
    hbm = pl.BlockSpec(memory_space=pl.ANY)
    dma = lambda *shape: pltpu.SemaphoreType.DMA(shape)
    return pl.pallas_call(
        kernel,
        out_shape=(
            jax.ShapeDtypeStruct((tokens, width), BF16),
            jax.ShapeDtypeStruct((own, width), BF16),
            jax.ShapeDtypeStruct((own, width), BF16),
            jax.ShapeDtypeStruct((d // (NZ * NY * NC), width), F32),
        ),
        in_specs=[smem, smem, smem, whole, hbm, hbm, hbm, hbm, hbm],
        out_specs=(whole,) * 4,
        scratch_shapes=[
            vmem(tokens, width), vmem(width, d), vmem(NX, patches, d), vmem(NX, patches, d),
            vmem(d, 512),
            vmem(NC, NY, own, width), vmem(NC, NZ, own, width),
            vmem(NZ, 8, 128, dtype=I32), vmem(NY, 8, 128, dtype=I32),
            vmem(512, 512), vmem(512, 512),
            vmem(NZ, 64, width), vmem(NY, 64, width), vmem(NZ, 64, width), vmem(NY, 64, width),
            vmem(tokens, width), vmem(tokens, width), vmem(NZ, 64, width), vmem(NY, 64, width),
            vmem(NC, NY, own, width), vmem(NC, NZ, own, width),
            vmem(NY, own, width), vmem(NZ, own, width),
            vmem(NY, own, width), vmem(NZ, own, width), vmem(NY, own, width), vmem(NZ, own, width),
            vmem(d, width), vmem(NZ, 144, width), vmem(NZ, 144, width),
            vmem(NY, 32, width), vmem(NY, 32, width),
            dma(5), dma(9), dma(9), dma(NX), dma(NX),
            dma(6, NZ), dma(6, NZ), dma(6, NY), dma(6, NY),
        ],
        compiler_params=pltpu.CompilerParams(
            collective_id=0, has_side_effects=True, vmem_limit_bytes=48 << 20
        ),
        name="routed_attention_backward",
    )(counts, source, offsets, key_mask, grad_out, queries, keys, values, out_weight)


def solution(mesh):
    in_specs = (
        P(("dp", "mp"), None),
        P("dp", "mp"),
        P("dp", "mp"),
        P("dp", "mp"),
        P("mp", None),
        P("dp"),
        P("dp"),
        P("dp"),
        P("dp", None),
    )
    out_specs = (P("dp", "mp"), P("dp", "mp"), P("dp", "mp"), P("dp", "mp"))
    return jax.shard_map(
        on_device, mesh=mesh, in_specs=in_specs, out_specs=out_specs, check_vma=False
    )
```

time: 519 us -> 89.4 us (0.17)
  waiting for transfers between devices: 396 us -> 0 us
  Pallas kernels: 0 us -> 78.4 us
  blocking collectives: 46.1 us -> 0 us
  starting transfers between devices: 17.8 us -> 0 us
  between operations: 18.1 us -> 1.3 us
  matrix products: 11.9 us -> 0 us
  local copies, waits for them, and re-layouts: 18.9 us -> 9.33 us
  other arithmetic: 8.56 us -> 0 us
    all_gather x3 -> x0, waiting for transfers between devices: 199 us -> none  [the longest x1 86.8 us: on_device(): lax.all_gather(keys, 'dp', axis=0, tiled=True)]
    unnamed x5 -> x0, waiting for transfers between devices: 164 us -> none
    pallas_call x0 -> x1, Pallas kernels: none -> 78.4 us  [on_device(): pl.pallas_call(kernel, out_shape=(jax.ShapeDtypeStruct((tokens, width), B...]
    unnamed x1 -> x0, blocking collectives: 46.1 us -> none
    all_to_all x2 -> x0, waiting for transfers between devices: 32 us -> none  [the longest x1 32 us: on_device(): lax.all_to_all(send_value_grads, 'dp', split_axis=0, concat_axis=0, tiled...]
    all_to_all x2 -> x0, starting transfers between devices: 17.5 us -> none  [the longest x1 9.58 us: on_device(): lax.all_to_all(send_value_grads, 'dp', split_axis=0, concat_axis=0, tiled...]
    dot_general x10 -> x0, matrix products: 11.9 us -> none  [the longest x1 3.69 us: on_device(): lax.dot_general(upstream, attended_rows, (((0,), (0,)), ((), ())), prefer...]
    gather x2 -> x0, local copies, waits for them, and re-layouts: 5.98 us -> none  [pick_rows(): taken = jnp.take(piece, safe, axis=0).reshape(held.shape)]
  transfers between devices with their start and end apart: 6 -> 0, of which waited for: 5 -> 0; matrix products, arithmetic and copies ran while one was open for 5% -> 0% of each run, Pallas kernels for 0% -> 0%
where the time goes in v1:
time: 89.4 us; the launch traced here: 89 us
  Pallas kernels  78.4 us (88%)
  local copies, waits for them, and re-layouts  9.33 us (10%)
  between operations  1.3 us (1%)
    pallas_call x1, Pallas kernels, on_device(): pl.pallas_call(kernel, out_shape=(jax.ShapeDtypeStruct((tokens, width), B...  78.4 us
    unnamed x20, local copies, waits for them, and re-layouts  9.33 us

profile of v1, /device:TPU:1, one launch (start us, length us, event | category | flops | bytes accessed | tf_op | source)
XLA Modules:
  0.0 89.0 jit_solution(11219834213047826744)
XLA Ops:
  1.3 0.0 copy-start
  1.3 1.5 %copy-done = bf16[384,2304]{1,0:T(8,128)(2,1)S(1)} copy-done((bf16[384,2304]{1,0:T(8,128)(2,1)S(1)}, bf16[384,2304]{1,0:T(8,128)(2,1)}, u32[]{:S(2)}) %copy-start) | copy-done | bytes 1769496
  2.8 0.0 copy-start.1
  2.8 1.0 %copy-done.1 = bf16[64,2304]{1,0:T(8,128)(2,1)S(1)} copy-done((bf16[64,2304]{1,0:T(8,128)(2,1)S(1)}, bf16[64,2304]{1,0:T(8,128)(2,1)}, u32[]{:S(2)}) %copy-start.1) | copy-done | bytes 294936
  3.7 0.0 copy-start.2
  3.7 0.9 %copy-done.2 = bf16[256,384]{1,0:T(8,128)(2,1)S(1)} copy-done((bf16[256,384]{1,0:T(8,128)(2,1)S(1)}, bf16[256,384]{1,0:T(8,128)(2,1)}, u32[]{:S(2)}) %copy-start.2) | copy-done | bytes 196632
  4.6 0.0 copy-start.3
  4.6 0.7 copy-done.3
  5.4 0.0 copy-start.4
  5.4 0.7 copy-done.4
  6.1 0.0 copy-start.5
  6.1 0.7 copy-done.5
  6.8 0.0 copy-start.6
  6.8 0.7 copy-done.6
  7.5 0.0 copy-start.7
  7.5 0.7 copy-done.7
  8.1 78.4 %routed_attention_backward.1 = (bf16[256,384]{1,0:T(8,128)(2,1)S(1)}, bf16[32,384]{1,0:T(8,128)(2,1)S(1)}, bf16[32,384]{1,0:T(8,128)(2,1)S(1)}, f32[18,384]{1,0:T(8,128)S(1)}) custom-call(s32[1]{0:T(128)S(6)} %copy.17.counts, s32[4]{0:T(128)S(1)} %copy-done.6, s32[4]{0:T(128)S(1)} %copy-done.7, s32[4,16]{1,0:T(4,128)S(1)} %copy-done.5, ...), custom_call_target="tpu_custom_call" | custom-call | tf_op jit(solution)/shard_map/routed_attention_backward/pallas_call | solution.py:284
  86.5 0.7 copy.18
  87.2 0.6 copy.19
  87.8 0.6 copy.20
  88.4 0.6 copy.21
Async XLA Ops:
  1.3 1.5 %copy-start = (bf16[384,2304]{1,0:T(8,128)(2,1)S(1)}, bf16[384,2304]{1,0:T(8,128)(2,1)}, u32[]{:S(2)}) copy-start(bf16[384,2304]{1,0:T(8,128)(2,1)} %w_hbm.1) | copy-start | bytes 5308420
  2.8 1.0 %copy-start.1 = (bf16[64,2304]{1,0:T(8,128)(2,1)S(1)}, bf16[64,2304]{1,0:T(8,128)(2,1)}, u32[]{:S(2)}) copy-start(bf16[64,2304]{1,0:T(8,128)(2,1)} %g_hbm.1) | copy-start | bytes 884740
  3.7 0.9 %copy-start.2 = (bf16[256,384]{1,0:T(8,128)(2,1)S(1)}, bf16[256,384]{1,0:T(8,128)(2,1)}, u32[]{:S(2)}) copy-start(bf16[256,384]{1,0:T(8,128)(2,1)} %q_hbm.1) | copy-start | bytes 589828
  4.6 0.7 copy-start.3
  5.4 0.7 copy-start.4
  6.1 0.7 copy-start.5
  6.8 0.7 copy-start.6
  7.5 0.7 copy-start.7

commit v2 on v1

v2 whole, which is shorter than its diff:
```python
import functools

import jax
import jax.numpy as jnp
from jax import lax
from jax.experimental import pallas as pl
from jax.experimental.pallas import tpu as pltpu
from jax.sharding import PartitionSpec as P

HEAD_DIM = 128
NZ, NY, NC, NX = 8, 8, 2, 4
MESH = pl.DeviceIdType.MESH
F32, BF16, I32 = jnp.float32, jnp.bfloat16, jnp.int32
NN = (((1,), (0,)), ((), ()))
NT = (((1,), (1,)), ((), ()))
TN = (((0,), (0,)), ((), ()))


def dot(a, b, dims):
    return lax.dot_general(a, b, dims, preferred_element_type=F32)


def total(ref, slots):
    acc = ref[0].astype(F32)
    for i in range(1, slots):
        acc = acc + ref[i].astype(F32)
    return acc


def kernel(
    counts, source_h, offsets_h, mask_h, g_h, q_h, k_h, v_h, w_h,
    qg_out, kg_out, vg_out, wg_out,
    source, offsets, mask, q_v, w_v, g_all, g_other, gt,
    kv_own, rows, meta_own, meta, pick, sel, kv_in,
    att, att_other, back_own, back, spread, last,
    w_part, w_turn, w_turned, wz_send, wy_send, wz_in, wy_in, wz_pad, wy_pad, wz_last, wy_last,
    local_sem, pair_send, pair_recv, x_send, x_recv, send, recv, w_sent, w_recv,
):
    scale = HEAD_DIM ** -0.5
    dp, x = lax.axis_index("dp"), lax.axis_index("mp")
    z, y, c = lax.div(dp, NY * NC), lax.rem(lax.div(dp, NC), NY), lax.rem(dp, NC)
    slots, patches, cond, own = 4, 64, 16, 32
    width = q_v.shape[1]
    heads = width // HEAD_DIM

    def place(z, y, c):
        return ((z * NY + y) * NC + c, x)

    z_at = [lax.rem(z + k, NZ) for k in range(NZ)]
    y_at = [lax.rem(y + k, NY) for k in range(NY)]
    from_at = [jnp.where(c == 0, y_at[k], z_at[k]) for k in range(8)]
    to_at = [jnp.where(c == 0, z_at[k], y_at[k]) for k in range(8)]
    pair = place(z, y, 1 - c)
    x_peer = [((z * NY + y) * NC + c, lax.rem(x + k, NX)) for k in range(NX)]

    def on_z(k, core):
        return place(z_at[k], y, core)

    def on_y(k, core):
        return place(z, y_at[k], core)

    def on_from(k, core):
        return place(jnp.where(c == 0, z, z_at[k]), jnp.where(c == 0, y_at[k], y), core)

    def on_to(k, core):
        return place(jnp.where(c == 0, z_at[k], z), jnp.where(c == 0, y, y_at[k]), core)

    started = []

    def push(src, dst, sent, got, device):
        copy = pltpu.make_async_remote_copy(
            src_ref=src, dst_ref=dst, send_sem=sent, recv_sem=got,
            device_id=device, device_id_type=MESH,
        )
        copy.start()
        started.append(copy)
        return copy

    def expect(dst, got):
        pltpu.make_async_remote_copy(
            src_ref=dst, dst_ref=dst, send_sem=pair_send.at[0], recv_sem=got,
            device_id=pair, device_id_type=MESH,
        ).wait_recv()

    def load(i, src, dst):
        copy = pltpu.make_async_copy(src, dst, local_sem.at[i])
        copy.start()
        return copy

    int_loads = [load(1, source_h, source), load(2, offsets_h, offsets)]
    load_k = load(3, k_h, kv_own.at[0])
    load_v = load(4, v_h, kv_own.at[1])
    load_g = load(5, g_h, g_all.at[x])
    load_m = load(6, mask_h, mask)
    load_q = load(7, q_h, q_v)
    load_w = load(8, w_h, w_v)

    barrier = pltpu.get_barrier_semaphore()
    near = [pair] + x_peer[1:]
    for core in range(NC):
        near += [on_z(k, core) for k in range(1, NZ)] + [on_y(k, core) for k in range(1, NY)]
    for device in near:
        pl.semaphore_signal(barrier, inc=1, device_id=device, device_id_type=MESH)

    for copy in int_loads:
        copy.wait()
    lane = lax.broadcasted_iota(I32, (8, 128), 1)
    slot, row = (lane >> 4) & 3, lane & 15
    named = jnp.full((8, 128), -(1 << 20), I32)
    for j in range(slots):
        first = jnp.where(j < counts[0], source[j] * own + offsets[j], -(1 << 20))
        named = jnp.where(slot == j, first + row, named)
    meta_own[...] = named
    meta[to_at[0], c] = named
    load_k.wait()
    load_v.wait()
    rows[from_at[0], c] = kv_own[c]
    load_g.wait()
    pl.semaphore_wait(barrier, len(near))

    for k in range(1, 8):
        push(kv_own.at[0], rows.at[y, c], send.at[0, 0, k], recv.at[0, c, k], on_y(k, 0))
        push(kv_own.at[1], rows.at[z, c], send.at[0, 1, k], recv.at[0, c, k], on_z(k, 1))
    push(kv_own.at[1 - c], rows.at[to_at[0], c], send.at[0, 0, 0], recv.at[0, c, 0], pair)
    for k in range(1, 8):
        push(meta_own, meta.at[z, c], send.at[1, 0, k], recv.at[1, c, k], on_z(k, 0))
        push(meta_own, meta.at[y, c], send.at[1, 1, k], recv.at[1, c, k], on_y(k, 1))
    push(meta_own, meta.at[from_at[0], c], send.at[1, 0, 0], recv.at[1, c, 0], pair)
    x_sent = [
        push(g_all.at[x], g_all.at[x], x_send.at[k], x_recv.at[k], x_peer[k]) for k in range(1, NX)
    ]
    g_pair = [push(g_all.at[x], g_other.at[x], pair_send.at[0], pair_recv.at[0], pair)]

    def arrive(line, dst):
        for k in range(1, 8):
            for core in range(NC):
                expect(dst, recv.at[line, core, k])
        expect(dst, recv.at[line, 1 - c, 0])

    def arrive_w(line, dst):
        for k in range(1, 8):
            expect(dst, w_recv.at[line, k])

    arrive(1, meta_own)
    left = lax.broadcasted_iota(I32, (1, 128), 1) < 64
    rows_of = lax.broadcasted_iota(I32, (512, 128), 0)
    for p in range(8):
        ids = jnp.where(left, meta[p, 0, 0:1, :], meta[p, 1, 0:1, :])
        ids_z, ids_y = ids >> 9, (ids >> 6) & 7
        keep = (ids >= 0) & (jnp.where(c == 0, ids_z, ids_y) == to_at[0])
        local = jnp.where(keep, jnp.where(c == 0, ids_y, ids_z) * 64 + (ids & 63), -1)
        pick[:, 128 * p : 128 * (p + 1)] = jnp.where(rows_of == local, 1.0, 0.0).astype(BF16)

    arrive(0, kv_own.at[0])
    sel[...] = (
        dot(pick[...], rows[...].reshape(512, width), TN).astype(BF16).reshape(8, 2, 64, width)
    )
    for k in range(1, 8):
        for core in range(NC):
            push(
                sel.at[to_at[k], core], kv_in.at[c, to_at[0]],
                send.at[2, core, k], recv.at[2, c, k], on_to(k, core),
            )
    push(
        sel.at[to_at[0], 1 - c], kv_in.at[c, to_at[0]],
        send.at[2, 0, 0], recv.at[2, c, 0], pair,
    )
    kv_in[c, to_at[0]] = sel[to_at[0], c]

    for k in range(1, NX):
        x_sent[k - 1].wait_recv()
        came = lax.rem(x + NX - k, NX)
        g_pair.append(
            push(g_all.at[came], g_other.at[came], pair_send.at[k], pair_recv.at[k], pair)
        )
    load_w.wait()
    load_q.wait()
    load_m.wait()
    g = g_all[...].reshape(slots * patches, -1)
    ga = dot(g, w_v[...], NT).astype(BF16)
    gt[:, 0:256] = g.T
    for copy in g_pair:
        copy.wait_recv()
    gt[:, 256:512] = g_other[...].reshape(slots * patches, -1).T

    eye = lax.broadcasted_iota(I32, (cond, cond), 0) == lax.broadcasted_iota(I32, (cond, cond), 1)
    kept = jnp.concatenate(
        [
            jnp.sum(jnp.where(eye, mask[s : s + 1, :].astype(F32), 0.0), axis=1, keepdims=True)
            for s in range(slots)
        ],
        axis=0,
    )
    same_slot = (lax.broadcasted_iota(I32, (64, 256), 0) >> 4) == (
        lax.broadcasted_iota(I32, (64, 256), 1) >> 6
    )

    def grouped(a, op):
        a = a.reshape(slots, cond, 256)
        a = op(a, axis=1, keepdims=True)
        return jnp.broadcast_to(a, (slots, cond, 256)).reshape(64, 256)

    arrive(2, kv_in.at[0, 0])
    k_blocks = total(kv_in.at[0], 8).astype(BF16)
    v_blocks = total(kv_in.at[1], 8).astype(BF16)
    q = q_v[...]
    probs = []
    for h in range(heads):
        cols = slice(h * HEAD_DIM, (h + 1) * HEAD_DIM)
        scores = dot(k_blocks[:, cols], q[:, cols], NT) * scale
        scores = jnp.where(kept > 0.5, scores, -1e30)
        expos = jnp.exp(scores - grouped(scores, jnp.max))
        probs.append(jnp.where(same_slot, expos / grouped(expos, jnp.sum), 0.0))
        att[:, cols] = dot(probs[h].astype(BF16), v_blocks[:, cols], TN).astype(BF16)
    att_pair = push(att, att_other, pair_send.at[4], pair_recv.at[4], pair)

    dscores = []
    for h in range(heads):
        cols = slice(h * HEAD_DIM, (h + 1) * HEAD_DIM)
        probs_b = probs[h].astype(BF16)
        dprob = dot(v_blocks[:, cols], ga[:, cols], NT)
        delta = grouped(probs_b.astype(F32) * dprob, jnp.sum)
        dscore = (probs[h] * (dprob - delta)).astype(BF16)
        dscores.append(dscore)
        back_own[0, :, cols] = (dot(dscore, q[:, cols], NN) * scale).astype(BF16)
        back_own[1, :, cols] = dot(probs_b, ga[:, cols], NN).astype(BF16)
    for k in range(1, 8):
        push(back_own.at[0], back.at[z, c], send.at[3, 0, k], recv.at[3, c, k], on_z(k, 0))
        push(back_own.at[1], back.at[y, c], send.at[3, 1, k], recv.at[3, c, k], on_y(k, 1))
    push(back_own.at[1 - c], back.at[from_at[0], c], send.at[3, 0, 0], recv.at[3, c, 0], pair)
    back[to_at[0], c] = back_own[c]

    att_pair.wait_recv()
    for b in range(6):
        part = slice(b * 384, (b + 1) * 384)
        w_part[part, :] = (
            dot(gt[part, 0:256], att[...], NN) + dot(gt[part, 256:512], att_other[...], NN)
        ).astype(BF16)
    i = lax.broadcasted_iota(I32, (144, 288), 0)
    parity = jnp.where(
        lax.broadcasted_iota(I32, (144, 288), 1) == i + 18 * ((i * 3641) >> 16) + 18 * c, 1.0, 0.0
    ).astype(BF16)
    for b in range(NZ):
        part = dot(parity, w_part[b * 288 : (b + 1) * 288, :], NN)
        wz_send[b] = part[:, 0:256].astype(BF16)
        w_turn[b] = part[:, 256:384]
    wz_in[z] = wz_send[z]
    for k in range(1, NZ):
        push(wz_send.at[z_at[k]], wz_in.at[z], w_sent.at[0, k], w_recv.at[0, k], on_z(k, c))
    for b in range(NZ):
        for a in range(NY):
            w_turned[a, b * 18 : (b + 1) * 18, :] = w_turn[b, a * 18 : (a + 1) * 18, :]
    wy_send[...] = w_turned[...].astype(BF16)
    wy_in[y] = wy_send[y]
    for k in range(1, NY):
        push(wy_send.at[y_at[k]], wy_in.at[y], w_sent.at[1, k], w_recv.at[1, k], on_y(k, c))

    for h in range(heads):
        cols = slice(h * HEAD_DIM, (h + 1) * HEAD_DIM)
        qg_out[:, cols] = (dot(dscores[h], k_blocks[:, cols], TN) * scale).astype(BF16)

    arrive(3, back_own.at[0])
    spread[...] = (
        dot(pick[...], back[...].reshape(1024, width), NN).astype(BF16).reshape(8, 2, own, width)
    )
    for k in range(1, 8):
        for core in range(NC):
            push(
                spread.at[from_at[k], core], last.at[c, from_at[0]],
                send.at[4, core, k], recv.at[4, c, k], on_from(k, core),
            )
    push(
        spread.at[from_at[0], 1 - c], last.at[c, from_at[0]],
        send.at[4, 0, 0], recv.at[4, c, 0], pair,
    )
    last[c, from_at[0]] = spread[from_at[0], c]

    o = lax.broadcasted_iota(I32, (256, 144), 0)
    pad = jnp.where(
        ((o & 31) < 18) & (lax.broadcasted_iota(I32, (256, 144), 1) == (o >> 5) * 18 + (o & 31)),
        1.0, 0.0,
    ).astype(BF16)
    arrive_w(1, wy_in.at[0])
    wy_pad[...] = dot(pad, total(wy_in, NY).astype(BF16), NN).astype(BF16).reshape(8, 32, 128)
    wy_last[z] = wy_pad[z]
    for k in range(1, NZ):
        push(wy_pad.at[z_at[k]], wy_last.at[z], w_sent.at[2, k], w_recv.at[2, k], on_z(k, c))
    arrive_w(0, wz_in.at[0])
    wz_pad[...] = dot(pad, total(wz_in, NZ).astype(BF16), NN).astype(BF16).reshape(8, 32, 256)
    wz_last[y] = wz_pad[y]
    for k in range(1, NY):
        push(wz_pad.at[y_at[k]], wz_last.at[y], w_sent.at[3, k], w_recv.at[3, k], on_y(k, c))

    arrive(4, last.at[0, 0])
    kg_out[...] = total(last.at[0], 8).astype(BF16)
    vg_out[...] = total(last.at[1], 8).astype(BF16)
    arrive_w(2, wy_last.at[0])
    wg_out[:, 256:384] = total(wy_last, NZ)[0:18, :]
    arrive_w(3, wz_last.at[0])
    wg_out[:, 0:256] = total(wz_last, NY)[0:18, :]
    for copy in started:
        copy.wait_send()


def on_device(grad_out, queries, keys, values, out_weight, counts, source, offsets, key_mask):
    patches, d = grad_out.shape
    tokens, width = queries.shape
    own = keys.shape[0]
    slots, cond = key_mask.shape
    vmem = lambda *shape, dtype=BF16: pltpu.VMEM(shape, dtype)
    whole = pl.BlockSpec(memory_space=pltpu.VMEM)
    hbm = pl.BlockSpec(memory_space=pltpu.HBM)
    dma = lambda *shape: pltpu.SemaphoreType.DMA(shape)
    operands = (source, offsets, key_mask, grad_out, queries, keys, values, out_weight)
    operands = [pltpu.with_memory_space_constraint(a, pltpu.HBM) for a in operands]
    return pl.pallas_call(
        kernel,
        out_shape=(
            jax.ShapeDtypeStruct((tokens, width), BF16),
            jax.ShapeDtypeStruct((own, width), BF16),
            jax.ShapeDtypeStruct((own, width), BF16),
            jax.ShapeDtypeStruct((d // (NZ * NY * NC), width), F32),
        ),
        in_specs=[pl.BlockSpec(memory_space=pltpu.SMEM)] + [hbm] * 8,
        out_specs=(whole,) * 4,
        scratch_shapes=[
            pltpu.SMEM((slots,), I32), pltpu.SMEM((slots,), I32),
            vmem(slots, cond, dtype=I32),
            vmem(tokens, width), vmem(width, d), vmem(NX, patches, d), vmem(NX, patches, d),
            vmem(d, 512),
            vmem(2, own, width), vmem(8, NC, own, width),
            vmem(8, 128, dtype=I32), vmem(8, NC, 8, 128, dtype=I32),
            vmem(512, 1024), vmem(8, NC, 64, width), vmem(2, 8, 64, width),
            vmem(tokens, width), vmem(tokens, width),
            vmem(2, 64, width), vmem(8, NC, 64, width),
            vmem(8, NC, own, width), vmem(2, 8, own, width),
            vmem(d, width), vmem(NZ, 144, 128, dtype=F32), vmem(NY, 144, 128, dtype=F32),
            vmem(NZ, 144, 256), vmem(NY, 144, 128), vmem(NZ, 144, 256), vmem(NY, 144, 128),
            vmem(NY, 32, 256), vmem(NZ, 32, 128), vmem(NY, 32, 256), vmem(NZ, 32, 128),
            dma(9), dma(5), dma(5), dma(NX), dma(NX),
            dma(5, 2, 8), dma(5, 2, 8), dma(4, 8), dma(4, 8),
        ],
        compiler_params=pltpu.CompilerParams(
            collective_id=0, has_side_effects=True, vmem_limit_bytes=48 << 20
        ),
        name="routed_attention_backward",
    )(counts, *operands)


def solution(mesh):
    in_specs = (
        P(("dp", "mp"), None),
        P("dp", "mp"),
        P("dp", "mp"),
        P("dp", "mp"),
        P("mp", None),
        P("dp"),
        P("dp"),
        P("dp"),
        P("dp", None),
    )
    out_specs = (P("dp", "mp"), P("dp", "mp"), P("dp", "mp"), P("dp", "mp"))
    return jax.shard_map(
        on_device, mesh=mesh, in_specs=in_specs, out_specs=out_specs, check_vma=False
    )
```

time: 89.4 us -> 73.8 us (0.83)
  Pallas kernels: 78.4 us -> 69.8 us
  local copies, waits for them, and re-layouts: 9.33 us -> 2.51 us
    pallas_call x1, Pallas kernels: 78.4 us -> 69.8 us  [on_device(): pl.pallas_call(kernel, out_shape=(jax.ShapeDtypeStruct((tokens, width), B...]
    unnamed x20 -> x4, local copies, waits for them, and re-layouts: 9.33 us -> 2.51 us
where the time goes in v2:
time: 73.8 us; the launch traced here: 73.6 us
  Pallas kernels  69.8 us (95%)
  local copies, waits for them, and re-layouts  2.51 us (3%)
  between operations  1.29 us (2%)
    pallas_call x1, Pallas kernels, on_device(): pl.pallas_call(kernel, out_shape=(jax.ShapeDtypeStruct((tokens, width), B...  69.8 us
    unnamed x4, local copies, waits for them, and re-layouts  2.51 us

profile of v2, /device:TPU:1, one launch (start us, length us, event | category | flops | bytes accessed | tf_op | source)
XLA Modules:
  0.0 73.6 jit_solution(17305463977955777048)
XLA Ops:
  1.3 69.8 %routed_attention_backward.1 = (bf16[256,384]{1,0:T(8,128)(2,1)S(1)}, bf16[32,384]{1,0:T(8,128)(2,1)S(1)}, bf16[32,384]{1,0:T(8,128)(2,1)S(1)}, f32[18,384]{1,0:T(8,128)S(1)}) custom-call(s32[1]{0:T(128)S(6)} %copy.17.counts, s32[4]{0:T(128)} %source_h.1, s32[4]{0:T(128)} %offsets_h.1, s32[4,16]{1,0:T(4,128)} %mask_h.1, bf16[64,2304]{1,0:T(8,128)(2,1)} %g_h.1, ...), custom_call_target="tpu_custom_call" | custom-call | tf_op jit(solution)/shard_map/routed_attention_backward/pallas_call | solution.py:316
  71.1 0.7 copy.18
  71.8 0.6 copy.19
  72.4 0.6 copy.20
  73.0 0.6 copy.21

commit v3 on v2

--- a/solution.py
+++ b/solution.py
@@ -33,7 +33,7 @@
     source, offsets, mask, q_v, w_v, g_all, g_other, gt,
     kv_own, rows, meta_own, meta, pick, sel, kv_in,
     att, att_other, back_own, back, spread, last,
-    w_part, w_turn, w_turned, wz_send, wy_send, wz_in, wy_in, wz_pad, wy_pad, wz_last, wy_last,
+    w_part, w_turn, w_turned, wz_send, wy_send, wz_in, wy_in, wz_go, wy_go, wz_pad, wy_pad, wz_last, wy_last,
     local_sem, pair_send, pair_recv, x_send, x_recv, send, recv, w_sent, w_recv,
 ):
     scale = HEAD_DIM ** -0.5
@@ -65,6 +65,7 @@
     def on_to(k, core):
         return place(jnp.where(c == 0, z_at[k], z), jnp.where(c == 0, y, y_at[k]), core)
 
+    far_first = (4, 3, 5, 2, 6, 1, 7)
     started = []
 
     def push(src, dst, sent, got, device):
@@ -87,6 +88,13 @@
         copy.start()
         return copy
 
+    barrier = pltpu.get_barrier_semaphore()
+    near = [pair] + x_peer[1:]
+    for core in range(NC):
+        near += [on_z(k, core) for k in range(1, NZ)] + [on_y(k, core) for k in range(1, NY)]
+    for device in near:
+        pl.semaphore_signal(barrier, inc=1, device_id=device, device_id_type=MESH)
+
     int_loads = [load(1, source_h, source), load(2, offsets_h, offsets)]
     load_k = load(3, k_h, kv_own.at[0])
     load_v = load(4, v_h, kv_own.at[1])
@@ -94,13 +102,6 @@
     load_m = load(6, mask_h, mask)
     load_q = load(7, q_h, q_v)
     load_w = load(8, w_h, w_v)
-
-    barrier = pltpu.get_barrier_semaphore()
-    near = [pair] + x_peer[1:]
-    for core in range(NC):
-        near += [on_z(k, core) for k in range(1, NZ)] + [on_y(k, core) for k in range(1, NY)]
-    for device in near:
-        pl.semaphore_signal(barrier, inc=1, device_id=device, device_id_type=MESH)
 
     for copy in int_loads:
         copy.wait()
@@ -118,11 +119,11 @@
     load_g.wait()
     pl.semaphore_wait(barrier, len(near))
 
-    for k in range(1, 8):
+    for k in far_first:
         push(kv_own.at[0], rows.at[y, c], send.at[0, 0, k], recv.at[0, c, k], on_y(k, 0))
         push(kv_own.at[1], rows.at[z, c], send.at[0, 1, k], recv.at[0, c, k], on_z(k, 1))
     push(kv_own.at[1 - c], rows.at[to_at[0], c], send.at[0, 0, 0], recv.at[0, c, 0], pair)
-    for k in range(1, 8):
+    for k in far_first:
         push(meta_own, meta.at[z, c], send.at[1, 0, k], recv.at[1, c, k], on_z(k, 0))
         push(meta_own, meta.at[y, c], send.at[1, 1, k], recv.at[1, c, k], on_y(k, 1))
     push(meta_own, meta.at[from_at[0], c], send.at[1, 0, 0], recv.at[1, c, 0], pair)
@@ -155,7 +156,7 @@
     sel[...] = (
         dot(pick[...], rows[...].reshape(512, width), TN).astype(BF16).reshape(8, 2, 64, width)
     )
-    for k in range(1, 8):
+    for k in far_first:
         for core in range(NC):
             push(
                 sel.at[to_at[k], core], kv_in.at[c, to_at[0]],
@@ -224,11 +225,21 @@
         dscores.append(dscore)
         back_own[0, :, cols] = (dot(dscore, q[:, cols], NN) * scale).astype(BF16)
         back_own[1, :, cols] = dot(probs_b, ga[:, cols], NN).astype(BF16)
-    for k in range(1, 8):
+    for k in (1, 7):
         push(back_own.at[0], back.at[z, c], send.at[3, 0, k], recv.at[3, c, k], on_z(k, 0))
         push(back_own.at[1], back.at[y, c], send.at[3, 1, k], recv.at[3, c, k], on_y(k, 1))
     push(back_own.at[1 - c], back.at[from_at[0], c], send.at[3, 0, 0], recv.at[3, c, 0], pair)
     back[to_at[0], c] = back_own[c]
+
+    def pass_on(far):
+        for k, step in ((far, 1), (8 - far, 7)):
+            if far == 3 and step == 7:
+                continue
+            for core in range(NC):
+                expect(back_own.at[0], recv.at[3, core, k])
+                block = back.at[to_at[8 - k], core]
+                push(block, block, send.at[3, core, k + step - 8 * (step == 7)],
+                     recv.at[3, core, k + step - 8 * (step == 7)], on_to(step, c))
 
     att_pair.wait_recv()
     for b in range(6):
@@ -236,34 +247,60 @@
         w_part[part, :] = (
             dot(gt[part, 0:256], att[...], NN) + dot(gt[part, 256:512], att_other[...], NN)
         ).astype(BF16)
-    i = lax.broadcasted_iota(I32, (144, 288), 0)
-    parity = jnp.where(
-        lax.broadcasted_iota(I32, (144, 288), 1) == i + 18 * ((i * 3641) >> 16) + 18 * c, 1.0, 0.0
-    ).astype(BF16)
+    def parity(kept, first):
+        i = lax.broadcasted_iota(I32, (8 * kept, 288), 0)
+        a = sum((i >= kept * n).astype(I32) for n in range(1, 8))
+        row = i + (36 - kept) * a + 18 * c + first
+        return jnp.where(lax.broadcasted_iota(I32, (8 * kept, 288), 1) == row, 1.0, 0.0).astype(BF16)
+
+    all_18, low_8, high_10 = parity(18, 0), parity(8, 0), parity(10, 8)
     for b in range(NZ):
-        part = dot(parity, w_part[b * 288 : (b + 1) * 288, :], NN)
-        wz_send[b] = part[:, 0:256].astype(BF16)
-        w_turn[b] = part[:, 256:384]
-    wz_in[z] = wz_send[z]
-    for k in range(1, NZ):
-        push(wz_send.at[z_at[k]], wz_in.at[z], w_sent.at[0, k], w_recv.at[0, k], on_z(k, c))
+        part = w_part[b * 288 : (b + 1) * 288, :]
+        wz_send[b, 0:144, :] = dot(all_18, part[:, 0:128], NN).astype(BF16)
+        wz_send[b, 144:208, :] = dot(low_8, part[:, 128:256], NN).astype(BF16)
+        w_turn[b, 0:144, :] = dot(all_18, part[:, 256:384], NN)
+        w_turn[b, 144:224, :] = dot(high_10, part[:, 128:256], NN)
+
+    def first_hop(line, own_part, came, at, on):
+        push(own_part.at[at[4]], came.at[1], w_sent.at[line, 1], w_recv.at[line, 1], on(1, c))
+        push(own_part.at[at[5]], came.at[5], w_sent.at[line, 5], w_recv.at[line, 5], on(7, c))
+
+    def next_hop(line, own_part, came, going, at, on, hop):
+        for i, far, step in ((hop, 5 - hop, 1), (hop + 4, hop + 4, 7)):
+            if i > 7:
+                continue
+            expect(came.at[0], w_recv.at[line, i - 1])
+            going[i] = (came[i - 1].astype(F32) + own_part[at[far]].astype(F32)).astype(BF16)
+            push(going.at[i], came.at[i], w_sent.at[line, i], w_recv.at[line, i], on(step, c))
+
+    first_hop(0, wz_send, wz_in, z_at, on_z)
+    pass_on(1)
     for b in range(NZ):
         for a in range(NY):
             w_turned[a, b * 18 : (b + 1) * 18, :] = w_turn[b, a * 18 : (a + 1) * 18, :]
+            w_turned[a, 144 + b * 10 : 154 + b * 10, :] = w_turn[b, 144 + a * 10 : 154 + a * 10, :]
     wy_send[...] = w_turned[...].astype(BF16)
-    wy_in[y] = wy_send[y]
-    for k in range(1, NY):
-        push(wy_send.at[y_at[k]], wy_in.at[y], w_sent.at[1, k], w_recv.at[1, k], on_y(k, c))
-
+    first_hop(1, wy_send, wy_in, y_at, on_y)
+    next_hop(0, wz_send, wz_in, wz_go, z_at, on_z, 2)
+    next_hop(1, wy_send, wy_in, wy_go, y_at, on_y, 2)
+    pass_on(2)
+    next_hop(0, wz_send, wz_in, wz_go, z_at, on_z, 3)
+    next_hop(1, wy_send, wy_in, wy_go, y_at, on_y, 3)
+    pass_on(3)
     for h in range(heads):
         cols = slice(h * HEAD_DIM, (h + 1) * HEAD_DIM)
         qg_out[:, cols] = (dot(dscores[h], k_blocks[:, cols], TN) * scale).astype(BF16)
 
-    arrive(3, back_own.at[0])
+    next_hop(0, wz_send, wz_in, wz_go, z_at, on_z, 4)
+    next_hop(1, wy_send, wy_in, wy_go, y_at, on_y, 4)
+    for core in range(NC):
+        for k in (4, 5):
+            expect(back_own.at[0], recv.at[3, core, k])
+    expect(back_own.at[0], recv.at[3, 1 - c, 0])
     spread[...] = (
         dot(pick[...], back[...].reshape(1024, width), NN).astype(BF16).reshape(8, 2, own, width)
     )
-    for k in range(1, 8):
+    for k in far_first:
         for core in range(NC):
             push(
                 spread.at[from_at[k], core], last.at[c, from_at[0]],
@@ -275,29 +312,37 @@
     )
     last[c, from_at[0]] = spread[from_at[0], c]
 
-    o = lax.broadcasted_iota(I32, (256, 144), 0)
-    pad = jnp.where(
-        ((o & 31) < 18) & (lax.broadcasted_iota(I32, (256, 144), 1) == (o >> 5) * 18 + (o & 31)),
-        1.0, 0.0,
-    ).astype(BF16)
-    arrive_w(1, wy_in.at[0])
-    wy_pad[...] = dot(pad, total(wy_in, NY).astype(BF16), NN).astype(BF16).reshape(8, 32, 128)
+    def pad(tall, tail):
+        o = lax.broadcasted_iota(I32, (256, tall), 0)
+        a, i = o >> 5, o & 31
+        row = jnp.where(i < 18, 18 * a + i, jnp.where(i < 18 + tail, 126 + tail * a + i, -1))
+        return jnp.where(lax.broadcasted_iota(I32, (256, tall), 1) == row, 1.0, 0.0).astype(BF16)
+
+    def summed(line, came, mine):
+        expect(came.at[0], w_recv.at[line, 4])
+        expect(came.at[0], w_recv.at[line, 7])
+        return (came[4].astype(F32) + came[7].astype(F32) + mine.astype(F32)).astype(BF16)
+
+    wy_pad[...] = dot(pad(224, 10), summed(1, wy_in, wy_send[y]), NN).astype(BF16).reshape(8, 32, 128)
     wy_last[z] = wy_pad[z]
-    for k in range(1, NZ):
+    for k in far_first:
         push(wy_pad.at[z_at[k]], wy_last.at[z], w_sent.at[2, k], w_recv.at[2, k], on_z(k, c))
-    arrive_w(0, wz_in.at[0])
-    wz_pad[...] = dot(pad, total(wz_in, NZ).astype(BF16), NN).astype(BF16).reshape(8, 32, 256)
+    wz_pad[...] = dot(pad(208, 8), summed(0, wz_in, wz_send[z]), NN).astype(BF16).reshape(8, 32, 128)
     wz_last[y] = wz_pad[y]
-    for k in range(1, NY):
+    for k in far_first:
         push(wz_pad.at[y_at[k]], wz_last.at[y], w_sent.at[3, k], w_recv.at[3, k], on_y(k, c))
 
     arrive(4, last.at[0, 0])
     kg_out[...] = total(last.at[0], 8).astype(BF16)
     vg_out[...] = total(last.at[1], 8).astype(BF16)
     arrive_w(2, wy_last.at[0])
-    wg_out[:, 256:384] = total(wy_last, NZ)[0:18, :]
+    by_y = total(wy_last, NZ)
+    wg_out[:, 256:384] = by_y[0:18, :]
+    wg_out[8:18, 128:256] = by_y[18:28, :]
     arrive_w(3, wz_last.at[0])
-    wg_out[:, 0:256] = total(wz_last, NY)[0:18, :]
+    by_z = total(wz_last, NY)
+    wg_out[:, 0:128] = by_z[0:18, :]
+    wg_out[0:8, 128:256] = by_z[18:26, :]
     for copy in started:
         copy.wait_send()
 
@@ -334,9 +379,10 @@
             vmem(tokens, width), vmem(tokens, width),
             vmem(2, 64, width), vmem(8, NC, 64, width),
             vmem(8, NC, own, width), vmem(2, 8, own, width),
-            vmem(d, width), vmem(NZ, 144, 128, dtype=F32), vmem(NY, 144, 128, dtype=F32),
-            vmem(NZ, 144, 256), vmem(NY, 144, 128), vmem(NZ, 144, 256), vmem(NY, 144, 128),
-            vmem(NY, 32, 256), vmem(NZ, 32, 128), vmem(NY, 32, 256), vmem(NZ, 32, 128),
+            vmem(d, width), vmem(NZ, 224, 128, dtype=F32), vmem(NY, 224, 128, dtype=F32),
+            vmem(NZ, 208, 128), vmem(NY, 224, 128), vmem(NZ, 208, 128), vmem(NY, 224, 128),
+            vmem(NZ, 208, 128), vmem(NY, 224, 128),
+            vmem(NY, 32, 128), vmem(NZ, 32, 128), vmem(NY, 32, 128), vmem(NZ, 32, 128),
             dma(9), dma(5), dma(5), dma(NX), dma(NX),
             dma(5, 2, 8), dma(5, 2, 8), dma(4, 8), dma(4, 8),
         ],

time: 73.8 us -> 67.5 us (0.915)
  Pallas kernels: 69.8 us -> 62.9 us
    pallas_call x1, Pallas kernels: 69.8 us -> 62.9 us  [on_device(): pl.pallas_call(kernel, out_shape=(jax.ShapeDtypeStruct((tokens, width), B...]
where the time goes in v3:
time: 67.5 us; the launch traced here: 66.7 us
  Pallas kernels  62.9 us (93%)
  local copies, waits for them, and re-layouts  2.51 us (4%)
  between operations  1.29 us (2%)
    pallas_call x1, Pallas kernels, on_device(): pl.pallas_call(kernel, out_shape=(jax.ShapeDtypeStruct((tokens, width), B...  62.9 us
    unnamed x4, local copies, waits for them, and re-layouts  2.51 us

profile of v3, /device:TPU:1, one launch (start us, length us, event | category | flops | bytes accessed | tf_op | source)
XLA Modules:
  0.0 66.7 jit_solution(4743735578632549264)
XLA Ops:
  1.3 62.9 %routed_attention_backward.1 = (bf16[256,384]{1,0:T(8,128)(2,1)S(1)}, bf16[32,384]{1,0:T(8,128)(2,1)S(1)}, bf16[32,384]{1,0:T(8,128)(2,1)S(1)}, f32[18,384]{1,0:T(8,128)S(1)}) custom-call(s32[1]{0:T(128)S(6)} %copy.17.counts, s32[4]{0:T(128)} %source_h.1, s32[4]{0:T(128)} %offsets_h.1, s32[4,16]{1,0:T(4,128)} %mask_h.1, bf16[64,2304]{1,0:T(8,128)(2,1)} %g_h.1, ...), custom_call_target="tpu_custom_call" | custom-call | tf_op jit(solution)/shard_map/routed_attention_backward/pallas_call | solution.py:361
  64.2 0.7 %copy.18 = bf16[256,384]{1,0:T(8,128)(2,1)} copy(bf16[256,384]{1,0:T(8,128)(2,1)S(1)} %get-tuple-element.8) | data formatting | bytes 393216
  64.9 0.6 copy.19
  65.5 0.6 copy.20
  66.1 0.6 copy.21

commit v4 on v3

--- a/solution.py
+++ b/solution.py
@@ -29,9 +29,9 @@
 
 def kernel(
     counts, source_h, offsets_h, mask_h, g_h, q_h, k_h, v_h, w_h,
-    qg_out, kg_out, vg_out, wg_out,
+    out, wg_out,
     source, offsets, mask, q_v, w_v, g_all, g_other, gt,
-    kv_own, rows, meta_own, meta, pick, sel, kv_in,
+    kv_own, rows, meta_own, meta, pick, sel, sel_came, sel_sum, kv_in,
     att, att_other, back_own, back, spread, last,
     w_part, w_turn, w_turned, wz_send, wy_send, wz_in, wy_in, wz_go, wy_go, wz_pad, wy_pad, wz_last, wy_last,
     local_sem, pair_send, pair_recv, x_send, x_recv, send, recv, w_sent, w_recv,
@@ -156,17 +156,32 @@
     sel[...] = (
         dot(pick[...], rows[...].reshape(512, width), TN).astype(BF16).reshape(8, 2, 64, width)
     )
-    for k in far_first:
-        for core in range(NC):
-            push(
-                sel.at[to_at[k], core], kv_in.at[c, to_at[0]],
-                send.at[2, core, k], recv.at[2, c, k], on_to(k, core),
+    steps = ((0, 1, 2, 3, 4), (1, 7, 6, 5, 8))
+    parts = (pl.ds(0, 32), pl.ds(32, 32))
+    for core in range(NC):
+        for way, one, two, three, four in steps:
+            push(sel.at[to_at[4], core, parts[way]], sel_came.at[way, 1, core, parts[way]],
+                 send.at[2, core, four], recv.at[2, core, four], on_to(two, c))
+            push(sel.at[to_at[three], core], sel_came.at[way, 0, core],
+                 send.at[2, core, three], recv.at[2, core, three], on_to(one, c))
+    for core in range(NC):
+        for way, one, *_ in steps:
+            push(sel.at[to_at[one], core], kv_in.at[c, 1 + way],
+                 send.at[2, core, one], recv.at[2, c, one], on_to(one, core))
+    push(sel.at[to_at[0], 1 - c], kv_in.at[c, 0], send.at[2, 0, 0], recv.at[2, c, 0], pair)
+    kv_in[c, 0] = sel[to_at[0], c]
+    for core in range(NC):
+        for way, one, two, three, four in steps:
+            expect(sel_came.at[0, 0, 0], recv.at[2, core, three])
+            expect(sel_came.at[0, 0, 0, parts[0]], recv.at[2, core, four])
+            part, rest = parts[way], parts[1 - way]
+            sel_sum[way, core, part] = (
+                sel[to_at[two], core, part] + sel_came[way, 0, core, part]
+                + sel_came[way, 1, core, part]
             )
-    push(
-        sel.at[to_at[0], 1 - c], kv_in.at[c, to_at[0]],
-        send.at[2, 0, 0], recv.at[2, c, 0], pair,
-    )
-    kv_in[c, to_at[0]] = sel[to_at[0], c]
+            sel_sum[way, core, rest] = sel[to_at[two], core, rest] + sel_came[way, 0, core, rest]
+            push(sel_sum.at[way, core], kv_in.at[c, 3 + way],
+                 send.at[2, core, two], recv.at[2, c, two], on_to(two, core))
 
     for k in range(1, NX):
         x_sent[k - 1].wait_recv()
@@ -201,9 +216,12 @@
         a = op(a, axis=1, keepdims=True)
         return jnp.broadcast_to(a, (slots, cond, 256)).reshape(64, 256)
 
-    arrive(2, kv_in.at[0, 0])
-    k_blocks = total(kv_in.at[0], 8).astype(BF16)
-    v_blocks = total(kv_in.at[1], 8).astype(BF16)
+    for kind in range(2):
+        for k in (1, 7, 2, 6):
+            expect(kv_in.at[0, 0], recv.at[2, kind, k])
+    expect(kv_in.at[0, 0], recv.at[2, 1 - c, 0])
+    k_blocks = total(kv_in.at[0], 5).astype(BF16)
+    v_blocks = total(kv_in.at[1], 5).astype(BF16)
     q = q_v[...]
     probs = []
     for h in range(heads):
@@ -225,21 +243,20 @@
         dscores.append(dscore)
         back_own[0, :, cols] = (dot(dscore, q[:, cols], NN) * scale).astype(BF16)
         back_own[1, :, cols] = dot(probs_b, ga[:, cols], NN).astype(BF16)
-    for k in (1, 7):
+    for k in (2, 6, 1, 7):
         push(back_own.at[0], back.at[z, c], send.at[3, 0, k], recv.at[3, c, k], on_z(k, 0))
         push(back_own.at[1], back.at[y, c], send.at[3, 1, k], recv.at[3, c, k], on_y(k, 1))
     push(back_own.at[1 - c], back.at[from_at[0], c], send.at[3, 0, 0], recv.at[3, c, 0], pair)
     back[to_at[0], c] = back_own[c]
 
-    def pass_on(far):
-        for k, step in ((far, 1), (8 - far, 7)):
-            if far == 3 and step == 7:
-                continue
-            for core in range(NC):
+    def pass_on():
+        for core in range(NC):
+            for k, near, got, half, rest in ((2, 1, 3, 4, 0), (6, 7, 5, 8, 32)):
                 expect(back_own.at[0], recv.at[3, core, k])
                 block = back.at[to_at[8 - k], core]
-                push(block, block, send.at[3, core, k + step - 8 * (step == 7)],
-                     recv.at[3, core, k + step - 8 * (step == 7)], on_to(step, c))
+                part = block.at[pl.ds(rest, 32)]
+                push(block, block, send.at[3, core, got], recv.at[3, core, got], on_to(near, c))
+                push(part, part, send.at[3, core, half], recv.at[3, core, half], on_to(k, c))
 
     att_pair.wait_recv()
     for b in range(6):
@@ -261,41 +278,51 @@
         w_turn[b, 0:144, :] = dot(all_18, part[:, 256:384], NN)
         w_turn[b, 144:224, :] = dot(high_10, part[:, 128:256], NN)
 
-    def first_hop(line, own_part, came, at, on):
-        push(own_part.at[at[4]], came.at[1], w_sent.at[line, 1], w_recv.at[line, 1], on(1, c))
-        push(own_part.at[at[5]], came.at[5], w_sent.at[line, 5], w_recv.at[line, 5], on(7, c))
-
-    def next_hop(line, own_part, came, going, at, on, hop):
-        for i, far, step in ((hop, 5 - hop, 1), (hop + 4, hop + 4, 7)):
-            if i > 7:
-                continue
-            expect(came.at[0], w_recv.at[line, i - 1])
-            going[i] = (came[i - 1].astype(F32) + own_part[at[far]].astype(F32)).astype(BF16)
-            push(going.at[i], came.at[i], w_sent.at[line, i], w_recv.at[line, i], on(step, c))
+    def halves(tall):
+        cut = tall // 32 * 16
+        return (pl.ds(0, cut), pl.ds(cut, tall - cut))
+
+    def first_hop(line, parts, came, at, on):
+        for base, near, two, part in zip((0, 4), (1, 7), (2, 6), halves(parts.shape[1])):
+            push(parts.at[at[4], part], came.at[base + 2, part],
+                 w_sent.at[line, base + 2], w_recv.at[line, base + 2], on(two, c))
+            push(parts.at[at[3 * near % 8]], came.at[base + 1],
+                 w_sent.at[line, base + 1], w_recv.at[line, base + 1], on(near, c))
+        for base, near in ((0, 1), (4, 7)):
+            push(parts.at[at[near]], came.at[base],
+                 w_sent.at[line, base], w_recv.at[line, base], on(near, c))
+
+    def next_hop(line, parts, came, going, at, on):
+        for base, two, part in zip((0, 4), (2, 6), halves(parts.shape[1])):
+            expect(came.at[0], w_recv.at[line, base + 1])
+            expect(came.at[0, part], w_recv.at[line, base + 2])
+            going[base] = came[base + 1] + parts[at[two]]
+            going[base, part] = (
+                came[base + 1, part].astype(F32) + parts[at[two], part].astype(F32)
+                + came[base + 2, part].astype(F32)
+            ).astype(BF16)
+            push(going.at[base], came.at[base + 3],
+                 w_sent.at[line, base + 3], w_recv.at[line, base + 3], on(two, c))
 
     first_hop(0, wz_send, wz_in, z_at, on_z)
-    pass_on(1)
     for b in range(NZ):
         for a in range(NY):
             w_turned[a, b * 18 : (b + 1) * 18, :] = w_turn[b, a * 18 : (a + 1) * 18, :]
             w_turned[a, 144 + b * 10 : 154 + b * 10, :] = w_turn[b, 144 + a * 10 : 154 + a * 10, :]
     wy_send[...] = w_turned[...].astype(BF16)
     first_hop(1, wy_send, wy_in, y_at, on_y)
-    next_hop(0, wz_send, wz_in, wz_go, z_at, on_z, 2)
-    next_hop(1, wy_send, wy_in, wy_go, y_at, on_y, 2)
-    pass_on(2)
-    next_hop(0, wz_send, wz_in, wz_go, z_at, on_z, 3)
-    next_hop(1, wy_send, wy_in, wy_go, y_at, on_y, 3)
-    pass_on(3)
+    pass_on()
+    next_hop(0, wz_send, wz_in, wz_go, z_at, on_z)
+    next_hop(1, wy_send, wy_in, wy_go, y_at, on_y)
     for h in range(heads):
         cols = slice(h * HEAD_DIM, (h + 1) * HEAD_DIM)
-        qg_out[:, cols] = (dot(dscores[h], k_blocks[:, cols], TN) * scale).astype(BF16)
-
-    next_hop(0, wz_send, wz_in, wz_go, z_at, on_z, 4)
-    next_hop(1, wy_send, wy_in, wy_go, y_at, on_y, 4)
+        out[0:256, cols] = (dot(dscores[h], k_blocks[:, cols], TN) * scale).astype(BF16)
+
     for core in range(NC):
-        for k in (4, 5):
+        for k in (1, 7, 3, 5):
             expect(back_own.at[0], recv.at[3, core, k])
+        for k in (4, 8):
+            expect(back_own.at[0, pl.ds(0, 32)], recv.at[3, core, k])
     expect(back_own.at[0], recv.at[3, 1 - c, 0])
     spread[...] = (
         dot(pick[...], back[...].reshape(1024, width), NN).astype(BF16).reshape(8, 2, own, width)
@@ -319,9 +346,11 @@
         return jnp.where(lax.broadcasted_iota(I32, (256, tall), 1) == row, 1.0, 0.0).astype(BF16)
 
     def summed(line, came, mine):
-        expect(came.at[0], w_recv.at[line, 4])
-        expect(came.at[0], w_recv.at[line, 7])
-        return (came[4].astype(F32) + came[7].astype(F32) + mine.astype(F32)).astype(BF16)
+        for i in (0, 3, 4, 7):
+            expect(came.at[0], w_recv.at[line, i])
+            mine = mine.astype(F32) + came[i].astype(F32)
+        return mine.astype(BF16)
+
 
     wy_pad[...] = dot(pad(224, 10), summed(1, wy_in, wy_send[y]), NN).astype(BF16).reshape(8, 32, 128)
     wy_last[z] = wy_pad[z]
@@ -333,8 +362,8 @@
         push(wz_pad.at[y_at[k]], wz_last.at[y], w_sent.at[3, k], w_recv.at[3, k], on_y(k, c))
 
     arrive(4, last.at[0, 0])
-    kg_out[...] = total(last.at[0], 8).astype(BF16)
-    vg_out[...] = total(last.at[1], 8).astype(BF16)
+    out[256:288, :] = total(last.at[0], 8).astype(BF16)
+    out[288:320, :] = total(last.at[1], 8).astype(BF16)
     arrive_w(2, wy_last.at[0])
     by_y = total(wy_last, NZ)
     wg_out[:, 256:384] = by_y[0:18, :]
@@ -358,16 +387,14 @@
     dma = lambda *shape: pltpu.SemaphoreType.DMA(shape)
     operands = (source, offsets, key_mask, grad_out, queries, keys, values, out_weight)
     operands = [pltpu.with_memory_space_constraint(a, pltpu.HBM) for a in operands]
-    return pl.pallas_call(
+    packed, wg = pl.pallas_call(
         kernel,
         out_shape=(
-            jax.ShapeDtypeStruct((tokens, width), BF16),
-            jax.ShapeDtypeStruct((own, width), BF16),
-            jax.ShapeDtypeStruct((own, width), BF16),
+            jax.ShapeDtypeStruct((tokens + 2 * own, width), BF16),
             jax.ShapeDtypeStruct((d // (NZ * NY * NC), width), F32),
         ),
         in_specs=[pl.BlockSpec(memory_space=pltpu.SMEM)] + [hbm] * 8,
-        out_specs=(whole,) * 4,
+        out_specs=(whole,) * 2,
         scratch_shapes=[
             pltpu.SMEM((slots,), I32), pltpu.SMEM((slots,), I32),
             vmem(slots, cond, dtype=I32),
@@ -375,7 +402,8 @@
             vmem(d, 512),
             vmem(2, own, width), vmem(8, NC, own, width),
             vmem(8, 128, dtype=I32), vmem(8, NC, 8, 128, dtype=I32),
-            vmem(512, 1024), vmem(8, NC, 64, width), vmem(2, 8, 64, width),
+            vmem(512, 1024), vmem(8, NC, 64, width),
+            vmem(2, 2, NC, 64, width), vmem(2, NC, 64, width), vmem(2, 5, 64, width),
             vmem(tokens, width), vmem(tokens, width),
             vmem(2, 64, width), vmem(8, NC, 64, width),
             vmem(8, NC, own, width), vmem(2, 8, own, width),
@@ -384,13 +412,14 @@
             vmem(NZ, 208, 128), vmem(NY, 224, 128),
             vmem(NY, 32, 128), vmem(NZ, 32, 128), vmem(NY, 32, 128), vmem(NZ, 32, 128),
             dma(9), dma(5), dma(5), dma(NX), dma(NX),
-            dma(5, 2, 8), dma(5, 2, 8), dma(4, 8), dma(4, 8),
+            dma(5, 2, 9), dma(5, 2, 9), dma(4, 8), dma(4, 8),
         ],
         compiler_params=pltpu.CompilerParams(
             collective_id=0, has_side_effects=True, vmem_limit_bytes=48 << 20
         ),
         name="routed_attention_backward",
     )(counts, *operands)
+    return packed[:tokens], packed[tokens : tokens + own], packed[tokens + own :], wg
 
 
 def solution(mesh):

time: 67.5 us -> 62 us (0.919)
  the two profiles are of different devices: /device:TPU:1 before, /device:TPU:6 now
where the time goes in v4:
time: 62 us; the launch traced here: 61.8 us
  Pallas kernels  58.6 us (95%)
  local copies, waits for them, and re-layouts  1.93 us (3%)
  between operations  1.29 us (2%)
    pallas_call x1, Pallas kernels, on_device(): pl.pallas_call(kernel, out_shape=(jax.ShapeDtypeStruct((tokens + 2 * own,...  58.6 us

profile of v4, /device:TPU:6, one launch (start us, length us, event | category | flops | bytes accessed | tf_op | source)
XLA Modules:
  0.0 61.8 jit_solution(9691659420821720892)
XLA Ops:
  1.3 58.6 %routed_attention_backward.1 = (bf16[320,384]{1,0:T(8,128)(2,1)S(1)}, f32[18,384]{1,0:T(8,128)S(1)}) custom-call(s32[1]{0:T(128)S(6)} %copy.14.counts, s32[4]{0:T(128)} %source_h.1, s32[4]{0:T(128)} %offsets_h.1, s32[4,16]{1,0:T(4,128)} %mask_h.1, bf16[64,2304]{1,0:T(8,128)(2,1)} %g_h.1, bf16[256,384]{1,0:T(8,128)(2,1)} %q_h.1, bf16[32,384]{1,0:T(8,128)(2,1)} %k_h.1, ...), custom_call_target="tpu_custom_call" | custom-call | tf_op jit(solution)/shard_map/routed_attention_backward/pallas_call | solution.py:390
  59.9 0.6 %fusion = (bf16[32,384]{1,0:T(8,128)(2,1)}, bf16[32,384]{1,0:T(8,128)(2,1)}) fusion(bf16[320,384]{1,0:T(8,128)(2,1)S(1)} %get-tuple-element.6), kind=kLoop, calls=%fused_computation | loop fusion | bytes 98304 | tf_op jit(solution)/shard_map/slice | solution.py:422
  60.5 0.7 %slice.9 = bf16[256,384]{1,0:T(8,128)(2,1)} slice(bf16[320,384]{1,0:T(8,128)(2,1)S(1)} %get-tuple-element.6), slice={[0:256], [0:384]} | slice | bytes 393216 | tf_op jit(solution)/shard_map/slice | solution.py:422
  61.2 0.6 copy.15

commit v5 on v4

--- a/solution.py
+++ b/solution.py
@@ -32,7 +32,7 @@
     out, wg_out,
     source, offsets, mask, q_v, w_v, g_all, g_other, gt,
     kv_own, rows, meta_own, meta, pick, sel, sel_came, sel_sum, kv_in,
-    att, att_other, back_own, back, spread, last,
+    att, att_other, back_own, back, spread, last_came, last_sum, last,
     w_part, w_turn, w_turned, wz_send, wy_send, wz_in, wy_in, wz_go, wy_go, wz_pad, wy_pad, wz_last, wy_last,
     local_sem, pair_send, pair_recv, x_send, x_recv, send, recv, w_sent, w_recv,
 ):
@@ -120,13 +120,13 @@
     pl.semaphore_wait(barrier, len(near))
 
     for k in far_first:
+        push(meta_own, meta.at[z, c], send.at[1, 0, k], recv.at[1, c, k], on_z(k, 0))
+        push(meta_own, meta.at[y, c], send.at[1, 1, k], recv.at[1, c, k], on_y(k, 1))
+    push(meta_own, meta.at[from_at[0], c], send.at[1, 0, 0], recv.at[1, c, 0], pair)
+    for k in far_first:
         push(kv_own.at[0], rows.at[y, c], send.at[0, 0, k], recv.at[0, c, k], on_y(k, 0))
         push(kv_own.at[1], rows.at[z, c], send.at[0, 1, k], recv.at[0, c, k], on_z(k, 1))
     push(kv_own.at[1 - c], rows.at[to_at[0], c], send.at[0, 0, 0], recv.at[0, c, 0], pair)
-    for k in far_first:
-        push(meta_own, meta.at[z, c], send.at[1, 0, k], recv.at[1, c, k], on_z(k, 0))
-        push(meta_own, meta.at[y, c], send.at[1, 1, k], recv.at[1, c, k], on_y(k, 1))
-    push(meta_own, meta.at[from_at[0], c], send.at[1, 0, 0], recv.at[1, c, 0], pair)
     x_sent = [
         push(g_all.at[x], g_all.at[x], x_send.at[k], x_recv.at[k], x_peer[k]) for k in range(1, NX)
     ]
@@ -327,17 +327,19 @@
     spread[...] = (
         dot(pick[...], back[...].reshape(1024, width), NN).astype(BF16).reshape(8, 2, own, width)
     )
-    for k in far_first:
-        for core in range(NC):
-            push(
-                spread.at[from_at[k], core], last.at[c, from_at[0]],
-                send.at[4, core, k], recv.at[4, c, k], on_from(k, core),
-            )
-    push(
-        spread.at[from_at[0], 1 - c], last.at[c, from_at[0]],
-        send.at[4, 0, 0], recv.at[4, c, 0], pair,
-    )
-    last[c, from_at[0]] = spread[from_at[0], c]
+    parts = (pl.ds(0, 16), pl.ds(16, 16))
+    for core in range(NC):
+        for way, one, two, three, four in steps:
+            push(spread.at[from_at[4], core, parts[way]], last_came.at[way, 1, core, parts[way]],
+                 send.at[4, core, four], recv.at[4, core, four], on_from(two, c))
+            push(spread.at[from_at[three], core], last_came.at[way, 0, core],
+                 send.at[4, core, three], recv.at[4, core, three], on_from(one, c))
+    for core in range(NC):
+        for way, one, *_ in steps:
+            push(spread.at[from_at[one], core], last.at[c, 1 + way],
+                 send.at[4, core, one], recv.at[4, c, one], on_from(one, core))
+    push(spread.at[from_at[0], 1 - c], last.at[c, 0], send.at[4, 0, 0], recv.at[4, c, 0], pair)
+    last[c, 0] = spread[from_at[0], c]
 
     def pad(tall, tail):
         o = lax.broadcasted_iota(I32, (256, tall), 0)
@@ -361,9 +363,24 @@
     for k in far_first:
         push(wz_pad.at[y_at[k]], wz_last.at[y], w_sent.at[3, k], w_recv.at[3, k], on_y(k, c))
 
-    arrive(4, last.at[0, 0])
-    out[256:288, :] = total(last.at[0], 8).astype(BF16)
-    out[288:320, :] = total(last.at[1], 8).astype(BF16)
+    for core in range(NC):
+        for way, one, two, three, four in steps:
+            expect(last_came.at[0, 0, 0], recv.at[4, core, three])
+            expect(last_came.at[0, 0, 0, parts[0]], recv.at[4, core, four])
+            part, rest = parts[way], parts[1 - way]
+            last_sum[way, core, part] = (
+                spread[from_at[two], core, part] + last_came[way, 0, core, part]
+                + last_came[way, 1, core, part]
+            )
+            last_sum[way, core, rest] = spread[from_at[two], core, rest] + last_came[way, 0, core, rest]
+            push(last_sum.at[way, core], last.at[c, 3 + way],
+                 send.at[4, core, two], recv.at[4, c, two], on_from(two, core))
+    for kind in range(2):
+        for k in (1, 7, 2, 6):
+            expect(last.at[0, 0], recv.at[4, kind, k])
+    expect(last.at[0, 0], recv.at[4, 1 - c, 0])
+    out[256:288, :] = total(last.at[0], 5).astype(BF16)
+    out[288:320, :] = total(last.at[1], 5).astype(BF16)
     arrive_w(2, wy_last.at[0])
     by_y = total(wy_last, NZ)
     wg_out[:, 256:384] = by_y[0:18, :]
@@ -406,7 +423,8 @@
             vmem(2, 2, NC, 64, width), vmem(2, NC, 64, width), vmem(2, 5, 64, width),
             vmem(tokens, width), vmem(tokens, width),
             vmem(2, 64, width), vmem(8, NC, 64, width),
-            vmem(8, NC, own, width), vmem(2, 8, own, width),
+            vmem(8, NC, own, width),
+            vmem(2, 2, NC, own, width), vmem(2, NC, own, width), vmem(2, 5, own, width),
             vmem(d, width), vmem(NZ, 224, 128, dtype=F32), vmem(NY, 224, 128, dtype=F32),
             vmem(NZ, 208, 128), vmem(NY, 224, 128), vmem(NZ, 208, 128), vmem(NY, 224, 128),
             vmem(NZ, 208, 128), vmem(NY, 224, 128),

time: 62 us -> 61.3 us (0.989)
  the two profiles are of different devices: /device:TPU:6 before, /device:TPU:1 now
where the time goes in v5:
time: 61.3 us; the launch traced here: 61.1 us
  Pallas kernels  57.9 us (94%)
  local copies, waits for them, and re-layouts  1.93 us (3%)
  between operations  1.29 us (2%)
    pallas_call x1, Pallas kernels, on_device(): pl.pallas_call(kernel, out_shape=(jax.ShapeDtypeStruct((tokens + 2 * own,...  57.9 us

profile of v5, /device:TPU:1, one launch (start us, length us, event | category | flops | bytes accessed | tf_op | source)
XLA Modules:
  0.0 61.1 jit_solution(1974637889343790042)
XLA Ops:
  1.3 57.9 %routed_attention_backward.1 = (bf16[320,384]{1,0:T(8,128)(2,1)S(1)}, f32[18,384]{1,0:T(8,128)S(1)}) custom-call(s32[1]{0:T(128)S(6)} %copy.14.counts, s32[4]{0:T(128)} %source_h.1, s32[4]{0:T(128)} %offsets_h.1, s32[4,16]{1,0:T(4,128)} %mask_h.1, bf16[64,2304]{1,0:T(8,128)(2,1)} %g_h.1, bf16[256,384]{1,0:T(8,128)(2,1)} %q_h.1, bf16[32,384]{1,0:T(8,128)(2,1)} %k_h.1, ...), custom_call_target="tpu_custom_call" | custom-call | tf_op jit(solution)/shard_map/routed_attention_backward/pallas_call | solution.py:407
  59.2 0.6 %fusion = (bf16[32,384]{1,0:T(8,128)(2,1)}, bf16[32,384]{1,0:T(8,128)(2,1)}) fusion(bf16[320,384]{1,0:T(8,128)(2,1)S(1)} %get-tuple-element.6), kind=kLoop, calls=%fused_computation | loop fusion | bytes 98304 | tf_op jit(solution)/shard_map/slice | solution.py:440
  59.8 0.7 %slice.9 = bf16[256,384]{1,0:T(8,128)(2,1)} slice(bf16[320,384]{1,0:T(8,128)(2,1)S(1)} %get-tuple-element.6), slice={[0:256], [0:384]} | slice | bytes 393216 | tf_op jit(solution)/shard_map/slice | solution.py:440
  60.5 0.6 %copy.15 = f32[18,384]{1,0:T(8,128)} copy(f32[18,384]{1,0:T(8,128)S(1)} %get-tuple-element.17) | data formatting | bytes 55296
